TPU v7x, 32 devices: a whole 2x2x4 slice. The times are simulated.
32 devices in a mesh: parts: 2 (over x), frames: 16 (over z, y, core).
Axes of the slice: x: 2, y: 2, z: 4, core: 2. Of those that a mesh axis runs over, the one named last changes fastest.
Arguments:
- tokens: bfloat16 [256, 64, 1024], P(('parts', 'frames')), parts along dimension 0, may hold values from -8 to 8
- gain_frame: float32 [1024], replicated, may hold values from 0.5 to 1.5
- qkv_frame: bfloat16 [1024, 1536], replicated, may hold values from -0.4 to 0.4
- out_frame: bfloat16 [512, 1024], replicated, may hold values from -0.25 to 0.25
- gain_global: float32 [1024], replicated, may hold values from 0.5 to 1.5
- qkv_global: bfloat16 [1024, 1536], replicated, may hold values from -0.4 to 0.4
- out_global: bfloat16 [512, 1024], replicated, may hold values from -4 to 4
- covis: int32 [256, 16], P(('parts', 'frames')), parts along dimension 0, may hold values from -1 to 127, as said below
- submap_ids: int32 [256], P(('parts', 'frames')), parts along dimension 0, may hold values from 0 to 7
- submap_anchor: int32 [16], P('parts'), parts along dimension 0, may hold values from 0 to 127
Outputs:
- frame_out: bfloat16 [256, 64, 1024], P(('parts', 'frames')), parts along dimension 0
- global_update: bfloat16 [256, 64, 1024], P(('parts', 'frames')), parts along dimension 0
There are 2 independent parts, one for each index of `parts`. A program takes and returns all parts, laid end to end along the dimension named above; an argument that names none is the same for every part. Nothing has to cross between parts.
Inputs may be any that keep to these rules, and one draw needn't show every extreme that they name: `covis`: block b holds frames b * 8 to b * 8 + 7. A frame's list holds distinct frames of other blocks, then -1 to the end. For any two different blocks d and b, exactly one frame of block d lists frames of block b, 1 to 2 of them. In every block one frame lists 16 frames.
All inputs are finite; a program needn't handle non-finite values.
Results may differ from a plain program's by a relative error of at most 0.014.
Values may be sent and summed in bfloat16 or wider, within the bound.
A program may use at most 192 MiB of HBM per device.

v0:
```python
import jax
import jax.numpy as jnp
from jax import lax
from jax.sharding import PartitionSpec as P

HEADS = 8
HD = 64
CAP_K = 2


masked_score = -1e30


def layer_norm(values, gain_vector):
    widened = values.astype(jnp.float32)
    centre = jnp.mean(widened, axis=-1, keepdims=True)
    variance = jnp.mean((widened - centre) ** 2, axis=-1, keepdims=True)
    return ((widened - centre) * lax.rsqrt(variance + 1e-06) * gain_vector).astype(jnp.bfloat16)


def split_heads(packed):
    return packed.reshape(packed.shape[:-1] + (HEADS, HD))


def per_row(statistic):
    return jnp.swapaxes(statistic, 1, 2)[..., None]


def partial_scores(queries, key_set, value_set, allowed):
    scores = jnp.einsum(
        "gqhd,gkhd->ghqk", queries, key_set, preferred_element_type=jnp.float32
    ) * HD ** (-0.5)
    visible = allowed[:, None, None, :]
    scores = jnp.where(visible, scores, masked_score)
    largest = jnp.max(scores, axis=-1)
    weights = jnp.where(visible, jnp.exp(scores - largest[..., None]), 0.0)
    totals = jnp.sum(weights, axis=-1)
    summed = jnp.einsum(
        "ghqk,gkhd->gqhd",
        weights.astype(jnp.bfloat16),
        value_set,
        preferred_element_type=jnp.float32,
    )
    return (summed, largest, totals)


def local(
    tokens,
    gain_frame,
    qkv_frame,
    out_frame,
    gain_global,
    qkv_global,
    out_global,
    covis,
    submap_ids,
    submap_anchor,
):
    frame_count, token_count, feature_count = tokens.shape
    row_count = frame_count * token_count
    inner_width = HEADS * HD
    block_count = lax.axis_size("frames")
    position = lax.axis_index("frames")
    normed = layer_norm(tokens.reshape(row_count, feature_count), gain_frame)
    packed = jnp.dot(normed, qkv_frame, preferred_element_type=jnp.float32).astype(jnp.bfloat16)
    packed = packed.reshape(frame_count, token_count, 3 * inner_width)
    everyone = jnp.ones((frame_count, token_count), bool)
    frame_sum, frame_top, frame_totals = partial_scores(
        split_heads(packed[..., :inner_width]),
        split_heads(packed[..., inner_width : 2 * inner_width]),
        split_heads(packed[..., 2 * inner_width :]),
        everyone,
    )
    attended = (frame_sum / per_row(frame_totals)).astype(jnp.bfloat16)
    frame_out = (
        tokens.reshape(row_count, feature_count).astype(jnp.float32)
        + jnp.dot(
            attended.reshape(row_count, inner_width), out_frame, preferred_element_type=jnp.float32
        )
    ).astype(jnp.bfloat16)
    normed_global = layer_norm(frame_out, gain_global)
    packed_global = jnp.dot(normed_global, qkv_global, preferred_element_type=jnp.float32).astype(
        jnp.bfloat16
    )
    packed_global = packed_global.reshape(frame_count, token_count, 3 * inner_width)
    queries_global = split_heads(packed_global[..., :inner_width])
    kv_local = packed_global[..., inner_width:]
    own_sum, own_top, own_totals = partial_scores(
        queries_global,
        split_heads(kv_local[..., :inner_width]),
        split_heads(kv_local[..., inner_width:]),
        everyone,
    )
    frame_range = jnp.arange(frame_count, dtype=jnp.int32)
    own_ids = position * frame_count + frame_range
    listed_ok = covis >= 0
    owners = jnp.where(listed_ok, covis // frame_count, -1)
    slot_index = covis % frame_count
    peer_ids = jnp.arange(block_count, dtype=jnp.int32)
    touches = owners[:, :, None] == peer_ids[None, None, :]
    asking = jnp.any(touches, axis=1).T
    has_peer = jnp.any(asking, axis=1)
    asker_index = jnp.sum(jnp.where(asking, frame_range[None, :], 0), axis=1)
    wanted_mask = jnp.any(
        touches[:, :, :, None] & (slot_index[:, :, None, None] == frame_range), axis=(0, 1)
    )
    before = jnp.cumsum(wanted_mask.astype(jnp.int32), axis=1) - 1
    slot_range = jnp.arange(CAP_K, dtype=jnp.int32)
    chosen = wanted_mask[:, :, None] & (before[:, :, None] == slot_range)
    request = jnp.where(
        jnp.any(chosen, axis=1),
        jnp.sum(jnp.where(chosen, frame_range[None, :, None], 0), axis=1),
        -1,
    )
    submap_range = jnp.arange(submap_anchor.shape[0], dtype=jnp.int32)
    anchor_ids = jnp.sum(
        jnp.where(submap_ids[:, None] == submap_range, submap_anchor[None, :], 0), axis=1
    )
    pair_queries = jnp.take(queries_global, asker_index, axis=0)
    asked = lax.all_to_all(request, "frames", split_axis=0, concat_axis=0, tiled=True)
    outgoing = jnp.take(kv_local, jnp.maximum(asked, 0), axis=0)
    fetched = lax.all_to_all(outgoing, "frames", split_axis=0, concat_axis=0, tiled=True)
    fetched = fetched.reshape(block_count, CAP_K * token_count, 2 * inner_width)
    allowed = request >= 0
    remote_sum, remote_top, remote_totals = partial_scores(
        pair_queries,
        split_heads(fetched[..., :inner_width]),
        split_heads(fetched[..., inner_width:]),
        jnp.repeat(allowed, token_count, axis=1),
    )
    holding = submap_anchor // frame_count == position
    selected = jnp.take(kv_local, submap_anchor % frame_count, axis=0)
    anchor_terms = jnp.where(holding[:, None, None], selected.astype(jnp.float32), 0.0)
    anchor_table = lax.psum(anchor_terms, "frames").astype(jnp.bfloat16)
    anchor_kv = jnp.take(anchor_table, submap_ids, axis=0)
    in_list = jnp.any(covis == anchor_ids[:, None], axis=1)
    anchor_ok = (anchor_ids != own_ids) & jnp.logical_not(in_list)
    anchor_sum, anchor_top, anchor_totals = partial_scores(
        queries_global,
        split_heads(anchor_kv[..., :inner_width]),
        split_heads(anchor_kv[..., inner_width:]),
        jnp.broadcast_to(anchor_ok[:, None], (frame_count, token_count)),
    )
    pair_top = jnp.max(
        jnp.where(asking[:, :, None, None], remote_top[:, None], masked_score), axis=0
    )
    overall = jnp.maximum(jnp.maximum(own_top, anchor_top), pair_top)
    pair_overall = jnp.take(overall, asker_index, axis=0)
    pair_factor = jnp.where(has_peer[:, None, None], jnp.exp(remote_top - pair_overall), 0.0)
    mixing = asking.astype(jnp.float32)
    pair_sum = jnp.einsum(
        "bf,bqhd->fqhd", mixing, remote_sum * per_row(pair_factor), precision=lax.Precision.HIGHEST
    )
    pair_totals = jnp.einsum(
        "bf,bhq->fhq", mixing, remote_totals * pair_factor, precision=lax.Precision.HIGHEST
    )
    own_factor = jnp.exp(own_top - overall)
    anchor_factor = jnp.exp(anchor_top - overall)
    numerator = own_sum * per_row(own_factor) + anchor_sum * per_row(anchor_factor) + pair_sum
    denominator = own_totals * own_factor + anchor_totals * anchor_factor + pair_totals
    attended_global = (numerator / per_row(denominator)).astype(jnp.bfloat16)
    global_update = jnp.dot(
        attended_global.reshape(row_count, inner_width),
        out_global,
        preferred_element_type=jnp.float32,
    ).astype(jnp.bfloat16)
    return (
        frame_out.reshape(frame_count, token_count, feature_count),
        global_update.reshape(frame_count, token_count, feature_count),
    )


def solution(mesh):
    return jax.shard_map(
        local,
        mesh=mesh,
        in_specs=(
            P(("parts", "frames"), None, None),
            P(),
            P(),
            P(),
            P(),
            P(),
            P(),
            P(("parts", "frames"), None),
            P(("parts", "frames")),
            P("parts"),
        ),
        out_specs=(P(("parts", "frames"), None, None), P(("parts", "frames"), None, None)),
        check_vma=False,
    )
```

profile of v0, /device:TPU:1, one launch (start us, length us, event | category | flops | bytes accessed | tf_op | source)
XLA Modules:
  0.0 262.5 jit_solution(8375255539915634801)
XLA Ops:
  2.7 7.3 %all-to-all-start = ((s32[16,1,2]{2,1,0:T(1,128)}), s32[16,1,2]{2,1,0:T(1,128)S(1)}, u32[]{:S(2)}, u32[]{:S(2)}) async-start(s32[16,1,2]{2,1,0:T(1,128)} %copy.141), calls=%async_computation | async-start | bytes 16384 | tf_op jit(solution)/shard_map/all_to_all | solution.py:120
  11.5 1.6 fusion.14
  13.3 1.6 fusion.17
  14.9 1.8 convolution_convert_fusion.1
  20.3 1.9 multiply_reduce_fusion.1
  23.4 1.5 fusion.12
  25.0 1.8 copy.130
  27.4 2.2 convert_reduce_fusion
  30.0 1.9 convolution_convert_fusion
  32.5 2.7 %gather_fusion.1 = bf16[32,64,1024]{2,1,0:T(8,128)(2,1)} fusion(bf16[8,64,1024]{2,1,0:T(8,128)(2,1)S(1)} %slice.62, s32[1024]{0:T(1024)S(1)} %pad_clamp_fusion), kind=kCustom, calls=%fused_computation.3 | custom fusion | bytes 8388736 | tf_op jit(solution)/shard_map/jit(_take)/gather | solution.py:121
  35.2 4.6 %broadcast_select_fusion = bf16[16,2,64,1024]{3,2,1,0:T(8,128)(2,1)} fusion(bf16[16,2,64,1024]{3,2,1,0:T(8,128)(2,1)} %bitcast.121, pred[16,2]{1,0:T(8,128)(4,1)S(1)} %copy.143), kind=kLoop, calls=%fused_computation.8 | loop fusion | flops 2097152 | bytes 8388640 | tf_op jit(solution)/shard_map/jit(_take)/select_n | solution.py:121
  39.9 6.1 %all-to-all-start.1 = ((bf16[16,2,64,1024]{3,2,1,0:T(8,128)(2,1)}), bf16[16,2,64,1024]{3,2,1,0:T(8,128)(2,1)}, u32[]{:S(2)}, u32[]{:S(2)}) async-start(bf16[16,2,64,1024]{3,2,1,0:T(8,128)(2,1)} %broadcast_select_fusion), calls=%async_computation.1 | async-start | bytes 8388608 | tf_op jit(solution)/shard_map/all_to_all | solution.py:122
  47.3 140.2 %all-reduce.1 = bf16[8,64,1024]{2,1,0:T(8,128)(2,1)S(1)} all-reduce(f32[8,64,1024]{2,1,0:T(8,128)S(1)} %convert_select_fusion), channel_id=1, replica_groups=mesh['parts'=2,'frames'=16] {'frames'}, use_global_device_ids=true, to_apply=%region_9.11 | all-reduce | flops 524288 | bytes 3145728 | tf_op jit(solution)/shard_map/psum | solution.py:134
  192.0 1.7 reshape.212
  193.7 2.4 reshape.213
  199.1 2.2 gather_fusion
  201.8 2.0 multiply_reduce_fusion
  205.4 1.6 broadcast_select_fusion.1
  207.4 1.8 fusion.36
  210.5 4.7 %fusion.87 = (bf16[16,128,512]{2,1,0:T(8,128)(2,1)}, bf16[16,128,512]{2,1,0:T(8,128)(2,1)}) fusion(bf16[16,128,1024]{2,1,0:T(8,128)(2,1)} %bitcast.17), kind=kLoop, calls=%fused_computation.163 | loop fusion | bytes 8388608 | tf_op jit(solution)/shard_map/slice | solution.py:127
  215.2 4.1 %copy.144 = bf16[16,128,512]{1,2,0:T(8,128)(2,1)} copy(bf16[16,128,512]{2,1,0:T(8,128)(2,1)} %get-tuple-element.7) | data formatting | bytes 4194304 | tf_op jit(solution)/shard_map/slice | solution.py:127
  219.2 4.7 %fusion = (f32[16,8,64]{2,1,0:T(8,128)S(1)}, f32[16,8,64,128]{3,2,1,0:T(8,128)}) fusion(pred[16,128]{1,0:T(8,128)(4,1)S(1)} %broadcast_in_dim.227, bf16[16,128,8,64]{1,3,2,0:T(8,128)(2,1)} %bitcast.122, bf16[16,64,8,64]{3,2,1,0:T(8,128)(2,1)S(1)} %copy-done.3), kind=kOutput, calls=%fused_computation.9 | convolution fusion | flops 137355264 | bytes 7374848 | tf_op jit(solution)/shard_map/gqhd,gkhd->ghqk/dot_general | solution.py:30
  224.7 4.1 %fusion.1 = f32[16,8,64]{2,1,0:T(8,128)S(1)} fusion(f32[16,8,64,128]{3,2,1,0:T(8,128)} %get-tuple-element.30, f32[16,8,64]{2,1,0:T(8,128)S(1)} %get-tuple-element.29, pred[16,128]{1,0:T(8,128)(4,1)S(1)} %broadcast_in_dim.227), kind=kLoop, calls=%fused_computation.12 | loop fusion | flops 5234688 | bytes 4261888 | tf_op jit(solution)/shard_map/reduce_sum | solution.py:37
  229.2 2.4 copy.151
  231.6 6.1 %bitcast_multiply_fusion = f32[16,64,8,64]{1,3,2,0:T(8,128)} fusion(bf16[16,128,8,64]{1,3,2,0:T(8,128)(2,1)} %bitcast.126, f32[16,8,64,128]{3,2,1,0:T(8,128)} %get-tuple-element.30, f32[16,64,8]{1,2,0:T(8,128)S(1)} %get-tuple-element.18, f32[16,8,64]{2,1,0:T(8,128)S(1)} %get-tuple-element.29, pred[16,128]{1,0:T(8,128)(4,1)S(1)} %broadcast_in_dim.227), kind=kOutput, calls=%fused_computation.5 | convolution fusion | flops 139984896 | bytes 8456192 | tf_op jit(solution)/shard_map/ghqk,gkhd->gqhd/dot_general | solution.py:38
  237.7 5.6 %copy.152 = f32[16,64,8,64]{3,0,2,1:T(8,128)} copy(f32[16,64,8,64]{1,3,2,0:T(8,128)} %bitcast_multiply_fusion) | data formatting | bytes 4194304 | tf_op jit(solution)/shard_map/mul | solution.py:152
  243.3 3.7 %fusion.71 = f32[8,64,8,64]{3,0,2,1:T(8,128)S(1)} fusion(f32[16,64,8,64]{3,0,2,1:T(8,128)} %copy.152, pred[8,16]{1,0:T(8,128)(4,1)S(1)} %get-tuple-element.4), kind=kOutput, calls=%fused_computation.127 | convolution fusion | flops 50331648 | bytes 3145856 | tf_op jit(solution)/shard_map/bf,bqhd->fqhd/dot_general | solution.py:151
  247.1 2.3 copy.153
  249.4 4.9 %fusion.25 = bf16[8,64,8,64]{1,3,2,0:T(8,128)(2,1)} fusion(f32[8,64,8,64]{1,3,2,0:T(8,128)} %copy.153, f32[8,8,64,64]{3,2,1,0:T(8,128)} %fusion.36, bf16[8,64,8,64]{1,3,2,0:T(8,128)(2,1)S(1)} %bitcast.128, f32[8,8,64,64]{2,3,1,0:T(8,128)} %copy-done.9, f32[8,64,8]{1,2,0:T(8,128)S(1)} %copy.157, f32[8,64,8]{1,2,0:T(8,128)S(1)} %copy.150, ...), kind=kOutput, calls=%fused_computation.49 | convolution fusion | flops 36438016 | bytes 4259848 | tf_op jit(solution)/shard_map/ghqk,gkhd->gqhd/dot_general | solution.py:38
  254.3 2.6 copy.158
  256.8 2.6 reshape.219
  259.4 3.1 %convolution_convert_fusion.2 = bf16[512,1024]{1,0:T(8,128)(2,1)} fusion(bf16[512,512]{1,0:T(8,128)(2,1)} %reshape.219, bf16[512,1024]{1,0:T(8,128)(2,1)} %param.18), kind=kOutput, calls=%fused_computation.59 | convolution fusion | flops 537395200 | bytes 2621440 | tf_op jit(solution)/shard_map/dot_general | solution.py:162
  (113 shorter events, 23.4 us)
Async XLA Ops:
  0.6 14.3 %copy-start = (bf16[1024,1536]{1,0:T(8,128)(2,1)S(1)}, bf16[1024,1536]{1,0:T(8,128)(2,1)}, u32[]{:S(2)}) copy-start(bf16[1024,1536]{1,0:T(8,128)(2,1)} %param.14) | copy-start | bytes 9437188
  0.6 12.6 %copy-start.16 = (f32[1024]{0:T(1024)S(1)}, f32[1024]{0:T(1024)}, u32[]{:S(2)}) copy-start(f32[1024]{0:T(1024)} %param.13) | copy-start | bytes 12292
  2.7 29.4 %all-to-all-start = ((s32[16,1,2]{2,1,0:T(1,128)}), s32[16,1,2]{2,1,0:T(1,128)S(1)}, u32[]{:S(2)}, u32[]{:S(2)}) async-start(s32[16,1,2]{2,1,0:T(1,128)} %copy.141), calls=%async_computation | async-start | bytes 16384 | tf_op jit(solution)/shard_map/all_to_all | solution.py:120
  22.2 1.2 copy-start.13
  25.0 2.4 copy-start.2
  27.4 2.6 %copy-start.18 = (bf16[1024,1536]{1,0:T(8,128)(2,1)S(1)}, bf16[1024,1536]{1,0:T(8,128)(2,1)}, u32[]{:S(2)}) copy-start(bf16[1024,1536]{1,0:T(8,128)(2,1)} %param.17) | copy-start | bytes 9437188
  27.4 2.6 %copy-start.19 = (f32[1024]{0:T(1024)S(1)}, f32[1024]{0:T(1024)}, u32[]{:S(2)}) copy-start(f32[1024]{0:T(1024)} %param.16) | copy-start | bytes 12292
  29.6 2.4 copy-start.14
  32.0 3.3 %copy-start.6 = (bf16[512,1536]{1,0:T(8,128)(2,1)}, bf16[512,1536]{1,0:T(8,128)(2,1)S(1)}, u32[]{:S(2)}) copy-start(bf16[512,1536]{1,0:T(8,128)(2,1)S(1)} %convolution_convert_fusion) | copy-start | bytes 4718596
  39.9 6.2 %copy-start.17 = (s32[8]{0:T(128)S(1)}, s32[8]{0:T(128)}, u32[]{:S(2)}) copy-start(s32[8]{0:T(128)} %param.21) | copy-start | bytes 100
  39.9 170.6 %all-to-all-start.1 = ((bf16[16,2,64,1024]{3,2,1,0:T(8,128)(2,1)}), bf16[16,2,64,1024]{3,2,1,0:T(8,128)(2,1)}, u32[]{:S(2)}, u32[]{:S(2)}) async-start(bf16[16,2,64,1024]{3,2,1,0:T(8,128)(2,1)} %broadcast_select_fusion), calls=%async_computation.1 | async-start | bytes 8388608 | tf_op jit(solution)/shard_map/all_to_all | solution.py:122
  46.7 0.7 copy-start.20
  188.4 2.5 copy-start.7
  192.0 5.8 %copy-start.10 = (bf16[8,64,512]{2,1,0:T(8,128)(2,1)S(1)}, bf16[8,64,512]{2,1,0:T(8,128)(2,1)}, u32[]{:S(2)}) copy-start(bf16[8,64,512]{2,1,0:T(8,128)(2,1)} %get-tuple-element.15) | copy-start | bytes 1572868
  199.1 2.4 copy-start.15
  201.7 2.0 copy-start.12
  203.8 1.6 copy-start.4
  205.4 3.7 %copy-start.9 = (f32[8,8,64,64]{2,3,1,0:T(8,128)}, f32[8,8,64,64]{2,3,1,0:T(8,128)S(1)}, u32[]{:S(2)}) copy-start(f32[8,8,64,64]{2,3,1,0:T(8,128)S(1)} %get-tuple-element.34) | copy-start | bytes 3145732
  205.4 2.0 copy-start.8
  215.2 4.1 %copy-start.3 = (bf16[16,64,8,64]{3,2,1,0:T(8,128)(2,1)S(1)}, bf16[16,64,8,64]{3,2,1,0:T(8,128)(2,1)}, u32[]{:S(2)}) copy-start(bf16[16,64,8,64]{3,2,1,0:T(8,128)(2,1)} %broadcast_select_fusion.1) | copy-start | bytes 3145732
  224.7 4.4 %copy-start.5 = (bf16[16,128,512]{2,1,0:T(8,128)(2,1)S(1)}, bf16[16,128,512]{2,1,0:T(8,128)(2,1)}, u32[]{:S(2)}) copy-start(bf16[16,128,512]{2,1,0:T(8,128)(2,1)} %get-tuple-element.8) | copy-start | bytes 6291460
  247.1 2.3 copy-start.11
  254.3 8.2 %copy-start.1 = (bf16[1024,1536]{1,0:T(8,128)(2,1)S(1)}, bf16[1024,1536]{1,0:T(8,128)(2,1)}, u32[]{:S(2)}) copy-start(bf16[1024,1536]{1,0:T(8,128)(2,1)} %param.14) | copy-start | bytes 9437188
where the time goes:
time: 268 us; the launch traced here: 262 us
  blocking collectives  140 us (52%)
  local copies, waits for them, and re-layouts  51 us (19%)
  matrix products  36.4 us (14%)
  other arithmetic  20.1 us (8%)
  starting transfers between devices  13.5 us (5%)
    psum x1, blocking collectives, local(): anchor_table = lax.psum(anchor_terms, 'frames').astype(jnp.bfloat16)  140 us
    dot_general x4, matrix products, partial_scores(): jnp.einsum('ghqk,gkhd->gqhd', weights.astype(jnp.bfloat16), value_set, pr...  14.3 us
    dot_general x4, matrix products, partial_scores(): jnp.einsum('gqhd,gkhd->ghqk', queries, key_set, preferred_element_type=jn...  9.28 us
    slice x2, local copies, waits for them, and re-layouts, local(): fetched[..., :inner_width]  8.71 us
    reshape x5, local copies, waits for them, and re-layouts, split_heads(): return packed.reshape(packed.shape[:-1] + (HEADS, HD))  7.65 us
    all_to_all x1, starting transfers between devices, local(): lax.all_to_all(request, 'frames', split_axis=0, concat_axis=0, tiled=True)  7.35 us
    all_to_all x1, starting transfers between devices, local(): lax.all_to_all(outgoing, 'frames', split_axis=0, concat_axis=0, tiled=True)  6.15 us
    reduce_sum x3, other arithmetic, partial_scores(): totals = jnp.sum(weights, axis=-1)  6.04 us
  transfers between devices with their start and end apart: 2, of which 0 were waited for; matrix products, arithmetic and copies ran while one was open for 17% of the time, Pallas kernels for 0%

commit v1 on v0

v1 whole, which is shorter than its diff:
```python
import functools

import jax
import jax.numpy as jnp
from jax import lax
from jax.experimental import pallas as pl
from jax.experimental.pallas import tpu as pltpu
from jax.sharding import PartitionSpec as P

HEADS = 8
HD = 64
CAP_K = 2
GROUP = 4
WIDE = GROUP * HD
EXTRA = 8
ANCHOR = "butterfly"

masked_score = -1e30


def layer_norm(widened, gain_row):
    centre = jnp.mean(widened, axis=-1, keepdims=True)
    shifted = widened - centre
    variance = jnp.mean(shifted * shifted, axis=-1, keepdims=True)
    return (shifted * lax.rsqrt(variance + 1e-06) * gain_row).astype(jnp.bfloat16)


def head_masks(rows):
    head = lax.broadcasted_iota(jnp.int32, (rows, WIDE), 1) // HD
    return [head == h for h in range(GROUP)]


def attend_group(queries, keys, values, masks, visible=None):
    zero = jnp.zeros_like(queries)
    stacked = jnp.concatenate([jnp.where(m, queries, zero) for m in masks], axis=0)
    scores = lax.dot_general(
        stacked, keys, (((1,), (1,)), ((), ())), preferred_element_type=jnp.float32
    ) * HD ** (-0.5)
    if visible is not None:
        scores = jnp.where(visible, scores, masked_score)
    largest = jnp.max(scores, axis=-1, keepdims=True)
    weights = jnp.exp(scores - largest)
    if visible is not None:
        weights = jnp.where(visible, weights, 0.0)
    totals = jnp.sum(weights, axis=-1, keepdims=True)
    totals = jnp.where(totals > 0.0, totals, 1.0)
    summed = jnp.dot(weights.astype(jnp.bfloat16), values, preferred_element_type=jnp.float32)
    summed = summed * (1.0 / totals)
    rows = queries.shape[0]
    out = jnp.where(masks[0], summed[:rows], 0.0)
    for h in range(1, GROUP):
        out = jnp.where(masks[h], summed[h * rows : (h + 1) * rows], out)
    return out, largest + jnp.log(totals)


def front_kernel(
    asker,
    request,
    holding,
    held,
    tokens,
    gain_frame,
    qkv_frame,
    out_frame,
    gain_global,
    qkv_global,
    frame_out,
    packed,
    message,
    anchors,
):
    step = pl.program_id(0)
    frames, length, features = tokens.shape
    inner = HEADS * HD
    rows = frames * length
    x = tokens[...].reshape(rows, features).astype(jnp.float32)
    normed = layer_norm(x, gain_frame[...])
    first = jnp.dot(normed, qkv_frame[...], preferred_element_type=jnp.float32).astype(
        jnp.bfloat16
    )
    masks = head_masks(length)
    attended = []
    for f in range(frames):
        mine = first[f * length : (f + 1) * length]
        parts = []
        for g in range(HEADS // GROUP):
            low = g * WIDE
            out, _ = attend_group(
                mine[:, low : low + WIDE],
                mine[:, inner + low : inner + low + WIDE],
                mine[:, 2 * inner + low : 2 * inner + low + WIDE],
                masks,
            )
            parts.append(out.astype(jnp.bfloat16))
        attended.append(jnp.concatenate(parts, axis=1))
    attended = jnp.concatenate(attended, axis=0)
    after = (
        x + jnp.dot(attended, out_frame[...], preferred_element_type=jnp.float32)
    ).astype(jnp.bfloat16)
    frame_out[...] = after.reshape(frames, length, features)
    normed = layer_norm(after.astype(jnp.float32), gain_global[...])
    second = jnp.dot(normed, qkv_global[...], preferred_element_type=jnp.float32).astype(
        jnp.bfloat16
    )
    packed[pl.ds(step * frames, frames)] = second.reshape(frames, length, 3 * inner)

    @pl.when(step == pl.num_programs(0) - 1)
    def _():
        row = lax.broadcasted_iota(jnp.int32, (EXTRA, inner), 0)
        lane = lax.broadcasted_iota(jnp.int32, (EXTRA, inner), 1)

        def put(b, carry):
            message[b, :length] = packed[asker[b], :, :inner]
            note = jnp.where(lane == 0, request[2 * b], jnp.where(lane == 1, request[2 * b + 1], 0))
            note = jnp.where(row == 0, note, 0)
            message[b, length:] = note.astype(jnp.float32).astype(jnp.bfloat16)
            return carry

        lax.fori_loop(0, message.shape[0], put, 0)

        def hold(s, carry):
            taken = packed[held[s], :, inner:]
            anchors[s] = jnp.where(holding[s] > 0, taken, jnp.zeros_like(taken))
            return carry

        lax.fori_loop(0, anchors.shape[0], hold, 0)


def split_three(values):
    high = values.astype(jnp.bfloat16)
    rest = values - high.astype(jnp.float32)
    middle = rest.astype(jnp.bfloat16)
    low = (rest - middle.astype(jnp.float32)).astype(jnp.bfloat16)
    return high, middle, low


def peer_kernel(asked, received, packed, reply):
    step = pl.program_id(0)
    per_step = received.shape[0]
    length = packed.shape[1]
    inner = HEADS * HD
    masks = head_masks(length)
    rows = GROUP * length
    second_half = lax.broadcasted_iota(jnp.int32, (1, 2 * length), 1) >= length
    eye = lax.broadcasted_iota(jnp.int32, (rows, rows), 0) == lax.broadcasted_iota(
        jnp.int32, (rows, rows), 1
    )
    note_row = lax.broadcasted_iota(jnp.int32, (EXTRA, rows), 0)
    for i in range(per_step):
        b = step * per_step + i
        one, two = asked[2 * b], asked[2 * b + 1]
        visible = jnp.where(second_half, two, one) >= 0
        one, two = jnp.maximum(one, 0), jnp.maximum(two, 0)
        for g in range(HEADS // GROUP):
            low = g * WIDE
            keys = jnp.concatenate(
                [packed[f, :, inner + low : inner + low + WIDE] for f in (one, two)], axis=0
            )
            values = jnp.concatenate(
                [packed[f, :, 2 * inner + low : 2 * inner + low + WIDE] for f in (one, two)],
                axis=0,
            )
            out, lse = attend_group(
                received[i, :length, low : low + WIDE], keys, values, masks, visible
            )
            reply[i, :length, low : low + WIDE] = out.astype(jnp.bfloat16)
            line = jnp.sum(jnp.where(eye, lse, 0.0), axis=0, keepdims=True)
            high, middle, small = [p.astype(jnp.float32) for p in split_three(line)]
            note = jnp.where(
                note_row == 0,
                high,
                jnp.where(note_row == 1, middle, jnp.where(note_row == 2, small, 0.0)),
            )
            reply[i, length:, low : low + WIDE] = note.astype(jnp.bfloat16)


def own_kernel(submap, anchor_ok, packed, table, out_ref, top_ref):
    step = pl.program_id(0)
    frames, length, _ = out_ref.shape
    inner = HEADS * HD
    masks = head_masks(length)
    second_half = lax.broadcasted_iota(jnp.int32, (1, 2 * length), 1) >= length
    for i in range(frames):
        f = step * frames + i
        s = submap[f]
        visible = jnp.where(second_half, anchor_ok[f], 1) > 0
        for g in range(HEADS // GROUP):
            low = g * WIDE
            keys = jnp.concatenate(
                [packed[f, :, inner + low : inner + low + WIDE], table[s, :, low : low + WIDE]],
                axis=0,
            )
            values = jnp.concatenate(
                [
                    packed[f, :, 2 * inner + low : 2 * inner + low + WIDE],
                    table[s, :, inner + low : inner + low + WIDE],
                ],
                axis=0,
            )
            out, lse = attend_group(
                packed[f, :, low : low + WIDE], keys, values, masks, visible
            )
            out_ref[i, :, low : low + WIDE] = out
            spread = jnp.where(masks[0], lse[:length], 0.0)
            for h in range(1, GROUP):
                spread = jnp.where(masks[h], lse[h * length : (h + 1) * length], spread)
            top_ref[i, :, low : low + WIDE] = spread


def merge_kernel(asker, has_peer, replies, own_out, own_top, out_global, update, acc, top, total):
    frames, length, inner = own_out.shape
    acc[...] = own_out[...]
    top[...] = own_top[...]
    total[...] = jnp.ones_like(total)
    rows = GROUP * length
    query_of = lax.broadcasted_iota(jnp.int32, (length, rows), 1) % length
    place = query_of == lax.broadcasted_iota(jnp.int32, (length, rows), 0)
    same_head = (
        lax.broadcasted_iota(jnp.int32, (rows, WIDE), 0) // length
        == lax.broadcasted_iota(jnp.int32, (rows, WIDE), 1) // HD
    )
    spreader = jnp.where(same_head, 1.0, 0.0).astype(jnp.bfloat16)

    def add(b, carry):
        @pl.when(has_peer[b] > 0)
        def _():
            f = asker[b]
            for g in range(HEADS // GROUP):
                cols = slice(g * WIDE, (g + 1) * WIDE)
                notes = replies[b, length:, cols].astype(jnp.float32)
                stacked = jnp.concatenate(
                    [
                        jnp.where(place, notes[k : k + 1], 0.0).astype(jnp.bfloat16)
                        for k in range(3)
                    ],
                    axis=0,
                )
                spread = jnp.dot(stacked, spreader, preferred_element_type=jnp.float32)
                lse = spread[:length] + spread[length : 2 * length] + spread[2 * length :]
                before = top[f, :, cols]
                largest = jnp.maximum(before, lse)
                keep, new = jnp.exp(before - largest), jnp.exp(lse - largest)
                top[f, :, cols] = largest
                total[f, :, cols] = total[f, :, cols] * keep + new
                acc[f, :, cols] = acc[f, :, cols] * keep + (
                    replies[b, :length, cols].astype(jnp.float32) * new
                )

        return carry

    lax.fori_loop(0, replies.shape[0], add, 0)
    attended = (acc[...] / total[...]).astype(jnp.bfloat16).reshape(frames * length, inner)
    update[...] = (
        jnp.dot(attended, out_global[...], preferred_element_type=jnp.float32)
        .astype(jnp.bfloat16)
        .reshape(update.shape)
    )


def whole(shape):
    return pl.BlockSpec(shape, lambda *_: (0,) * len(shape))


def share_anchors(terms, position, block_count):
    if ANCHOR == "psum":
        return lax.psum(terms, "frames")
    shape = terms.shape
    held = terms.reshape(shape[0] * shape[1], shape[2])
    if ANCHOR == "a2a":
        pieces = held.reshape(block_count, -1, shape[2])
        got = lax.all_to_all(pieces, "frames", split_axis=0, concat_axis=0, tiled=True)
        mine = jnp.sum(got.astype(jnp.float32), axis=0).astype(jnp.bfloat16)
        return lax.all_gather(mine, "frames", tiled=True).reshape(shape)
    bits = block_count.bit_length() - 1
    for bit in range(bits):
        half = held.shape[0] // 2
        mine = (position >> bit) & 1
        keep = lax.dynamic_slice_in_dim(held, mine * half, half, 0)
        send = lax.dynamic_slice_in_dim(held, (1 - mine) * half, half, 0)
        got = lax.ppermute(send, "frames", [(d, d ^ (1 << bit)) for d in range(block_count)])
        held = keep + got
    for bit in reversed(range(bits)):
        mine = (position >> bit) & 1
        got = lax.ppermute(held, "frames", [(d, d ^ (1 << bit)) for d in range(block_count)])
        held = jnp.concatenate(
            [jnp.where(mine == 0, held, got), jnp.where(mine == 0, got, held)], axis=0
        )
    return held.reshape(shape)


def local(
    tokens,
    gain_frame,
    qkv_frame,
    out_frame,
    gain_global,
    qkv_global,
    out_global,
    covis,
    submap_ids,
    submap_anchor,
):
    frame_count, token_count, feature_count = tokens.shape
    inner_width = HEADS * HD
    block_count = lax.axis_size("frames")
    position = lax.axis_index("frames")
    submap_count = submap_anchor.shape[0]

    frame_range = jnp.arange(frame_count, dtype=jnp.int32)
    own_ids = position * frame_count + frame_range
    listed_ok = covis >= 0
    owners = jnp.where(listed_ok, covis // frame_count, -1)
    slot_index = covis % frame_count
    peer_ids = jnp.arange(block_count, dtype=jnp.int32)
    touches = owners[:, :, None] == peer_ids[None, None, :]
    asker_index = jnp.max(jnp.where(touches, frame_range[:, None, None], 0), axis=(0, 1))
    lowest = jnp.min(jnp.where(touches, slot_index[:, :, None], frame_count), axis=(0, 1))
    highest = jnp.max(jnp.where(touches, slot_index[:, :, None], -1), axis=(0, 1))
    has_peer = (highest >= 0).astype(jnp.int32)
    request = jnp.stack(
        [
            jnp.where(has_peer > 0, lowest, -1),
            jnp.where((has_peer > 0) & (highest != lowest), highest, -1),
        ],
        axis=1,
    ).reshape(-1)
    submap_range = jnp.arange(submap_count, dtype=jnp.int32)
    anchor_ids = jnp.sum(
        jnp.where(submap_ids[:, None] == submap_range, submap_anchor[None, :], 0), axis=1
    )
    in_list = jnp.any(covis == anchor_ids[:, None], axis=1)
    anchor_ok = ((anchor_ids != own_ids) & jnp.logical_not(in_list)).astype(jnp.int32)
    holding = (submap_anchor // frame_count == position).astype(jnp.int32)
    held = submap_anchor % frame_count

    rows = token_count + EXTRA
    steps = 2
    each = frame_count // steps
    frame_out, packed, message, anchor_terms = pl.pallas_call(
        front_kernel,
        grid_spec=pltpu.PrefetchScalarGridSpec(
            num_scalar_prefetch=4,
            grid=(steps,),
            in_specs=[
                pl.BlockSpec((each, token_count, feature_count), lambda i, *_: (i, 0, 0)),
                whole((1, feature_count)),
                whole(qkv_frame.shape),
                whole(out_frame.shape),
                whole((1, feature_count)),
                whole(qkv_global.shape),
            ],
            out_specs=[
                pl.BlockSpec((each, token_count, feature_count), lambda i, *_: (i, 0, 0)),
                whole((frame_count, token_count, 3 * inner_width)),
                whole((block_count, rows, inner_width)),
                whole((submap_count, token_count, 2 * inner_width)),
            ],
        ),
        out_shape=[
            jax.ShapeDtypeStruct(tokens.shape, jnp.bfloat16),
            jax.ShapeDtypeStruct((frame_count, token_count, 3 * inner_width), jnp.bfloat16),
            jax.ShapeDtypeStruct((block_count, rows, inner_width), jnp.bfloat16),
            jax.ShapeDtypeStruct((submap_count, token_count, 2 * inner_width), jnp.bfloat16),
        ],
        compiler_params=pltpu.CompilerParams(vmem_limit_bytes=52 * 2**20),
        cost_estimate=pl.CostEstimate(
            flops=4 * 10**9, bytes_accessed=15 * 10**6, transcendentals=10**6
        ),
        name="front",
    )(
        asker_index,
        request,
        holding,
        held,
        tokens,
        gain_frame.reshape(1, -1),
        qkv_frame,
        out_frame,
        gain_global.reshape(1, -1),
        qkv_global,
    )

    received = lax.all_to_all(message, "frames", split_axis=0, concat_axis=0, tiled=True)
    table = share_anchors(anchor_terms, position, block_count)

    asked = received[:, token_count, :CAP_K].astype(jnp.int32).reshape(-1)
    per_step = 4
    reply = pl.pallas_call(
        peer_kernel,
        grid_spec=pltpu.PrefetchScalarGridSpec(
            num_scalar_prefetch=1,
            grid=(block_count // per_step,),
            in_specs=[
                pl.BlockSpec((per_step, rows, inner_width), lambda i, *_: (i, 0, 0)),
                whole(packed.shape),
            ],
            out_specs=pl.BlockSpec((per_step, rows, inner_width), lambda i, *_: (i, 0, 0)),
        ),
        out_shape=jax.ShapeDtypeStruct((block_count, rows, inner_width), jnp.bfloat16),
        compiler_params=pltpu.CompilerParams(vmem_limit_bytes=24 * 2**20),
        cost_estimate=pl.CostEstimate(
            flops=2 * 10**9, bytes_accessed=4 * 10**6, transcendentals=10**6
        ),
        name="peer",
    )(asked, received, packed)

    replies = lax.all_to_all(reply, "frames", split_axis=0, concat_axis=0, tiled=True)

    own_out, own_top = pl.pallas_call(
        own_kernel,
        grid_spec=pltpu.PrefetchScalarGridSpec(
            num_scalar_prefetch=2,
            grid=(steps,),
            in_specs=[whole(packed.shape), whole(table.shape)],
            out_specs=[
                pl.BlockSpec((each, token_count, inner_width), lambda i, *_: (i, 0, 0)),
                pl.BlockSpec((each, token_count, inner_width), lambda i, *_: (i, 0, 0)),
            ],
        ),
        out_shape=[
            jax.ShapeDtypeStruct((frame_count, token_count, inner_width), jnp.float32),
            jax.ShapeDtypeStruct((frame_count, token_count, inner_width), jnp.float32),
        ],
        compiler_params=pltpu.CompilerParams(vmem_limit_bytes=24 * 2**20),
        cost_estimate=pl.CostEstimate(
            flops=10**9, bytes_accessed=4 * 10**6, transcendentals=10**6
        ),
        name="own",
    )(submap_ids, anchor_ok, packed, table)

    global_update = pl.pallas_call(
        merge_kernel,
        grid_spec=pltpu.PrefetchScalarGridSpec(
            num_scalar_prefetch=2,
            grid=(1,),
            in_specs=[
                whole(replies.shape),
                whole(own_out.shape),
                whole(own_top.shape),
                whole(out_global.shape),
            ],
            out_specs=whole(tokens.shape),
            scratch_shapes=[pltpu.VMEM(own_out.shape, jnp.float32)] * 3,
        ),
        out_shape=jax.ShapeDtypeStruct(tokens.shape, jnp.bfloat16),
        compiler_params=pltpu.CompilerParams(vmem_limit_bytes=40 * 2**20),
        cost_estimate=pl.CostEstimate(
            flops=10**9, bytes_accessed=6 * 10**6, transcendentals=10**6
        ),
        name="merge",
    )(asker_index, has_peer, replies, own_out, own_top, out_global)
    return frame_out, global_update


def solution(mesh):
    return jax.shard_map(
        local,
        mesh=mesh,
        in_specs=(
            P(("parts", "frames"), None, None),
            P(),
            P(),
            P(),
            P(),
            P(),
            P(),
            P(("parts", "frames"), None),
            P(("parts", "frames")),
            P("parts"),
        ),
        out_specs=(P(("parts", "frames"), None, None), P(("parts", "frames"), None, None)),
        check_vma=False,
    )
```

time: 268 us -> 125 us (0.47); the launches traced: 262 us -> 123 us
  blocking collectives: 140 us -> 0 us
  waiting for transfers between devices: 0.01 us -> 60.5 us
  local copies, waits for them, and re-layouts: 51 us -> 5.25 us
  matrix products: 36.4 us -> 0 us
  Pallas kernels: 0 us -> 28.8 us
  other arithmetic: 20.1 us -> 4.41 us
  starting transfers between devices: 13.5 us -> 23.4 us
    psum x1 -> x0, blocking collectives: 140 us -> none  [local(): anchor_table = lax.psum(anchor_terms, 'frames').astype(jnp.bfloat16)]
    ppermute x0 -> x8, waiting for transfers between devices: none -> 60.5 us  [the longest x4 33.3 us: share_anchors(): lax.ppermute(held, 'frames', [(d, d ^ 1 << bit) for d in range(block_coun...]
    dot_general x14 -> x0, matrix products: 36.4 us -> none  [the longest x4 14.3 us: partial_scores(): jnp.einsum('ghqk,gkhd->gqhd', weights.astype(jnp.bfloat16), value_set, pr...]
    pallas_call x0 -> x4, Pallas kernels: none -> 28.8 us  [the longest x1 12.9 us: local(): pl.pallas_call(front_kernel, grid_spec=pltpu.PrefetchScalarGridSpec(num_s...]
    slice x10 -> x0, local copies, waits for them, and re-layouts: 17.5 us -> none  [the longest x2 8.71 us: local(): fetched[..., :inner_width]]
    reshape x7 -> x1, local copies, waits for them, and re-layouts: 10.8 us -> 0.09 us  [local(): request = jnp.stack([jnp.where(has_peer > 0, lowest, -1), jnp.where((has_...]
    reduce_sum x8 -> x0, other arithmetic: 9.56 us -> none  [the longest x3 6.04 us: partial_scores(): totals = jnp.sum(weights, axis=-1)]
    gather x5 -> x0, local copies, waits for them, and re-layouts: 6.74 us -> none  [the longest x1 2.74 us: local(): outgoing = jnp.take(kv_local, jnp.maximum(asked, 0), axis=0)]
  transfers between devices with their start and end apart: 2 -> 10, of which waited for: 0 -> 7; matrix products, arithmetic and copies ran while one was open for 17% -> 2% of each run, Pallas kernels for 0% -> 2%
where the time goes in v1:
time: 125 us; the launch traced here: 123 us
  waiting for transfers between devices  60.5 us (48%)
  Pallas kernels  28.8 us (23%)
  starting transfers between devices  23.4 us (19%)
  local copies, waits for them, and re-layouts  5.25 us (4%)
  other arithmetic  4.41 us (4%)
    ppermute x4, waiting for transfers between devices, share_anchors(): lax.ppermute(held, 'frames', [(d, d ^ 1 << bit) for d in range(block_coun...  33.3 us
    ppermute x4, waiting for transfers between devices, share_anchors(): lax.ppermute(send, 'frames', [(d, d ^ 1 << bit) for d in range(block_coun...  27.2 us
    pallas_call x1, Pallas kernels, local(): pl.pallas_call(front_kernel, grid_spec=pltpu.PrefetchScalarGridSpec(num_s...  12.9 us
    all_to_all x1, starting transfers between devices, local(): lax.all_to_all(reply, 'frames', split_axis=0, concat_axis=0, tiled=True)  10.1 us
    all_to_all x1, starting transfers between devices, local(): lax.all_to_all(message, 'frames', split_axis=0, concat_axis=0, tiled=True)  7.4 us
    pallas_call x1, Pallas kernels, local(): pl.pallas_call(peer_kernel, grid_spec=pltpu.PrefetchScalarGridSpec(num_sc...  6.55 us
    pallas_call x1, Pallas kernels, local(): pl.pallas_call(merge_kernel, grid_spec=pltpu.PrefetchScalarGridSpec(num_s...  6.39 us
    unnamed x20, local copies, waits for them, and re-layouts  4.9 us
  transfers between devices with their start and end apart: 10, of which 7 were waited for; matrix products, arithmetic and copies ran while one was open for 2% of the time, Pallas kernels for 2%

profile of v1, /device:TPU:1, one launch (start us, length us, event | category | flops | bytes accessed | tf_op | source)
XLA Modules:
  0.0 123.3 jit_solution(5918945805647389465)
XLA Ops:
  0.6 0.7 and_select_fusion.held
  1.3 0.7 compare_convert_fusion.1.holding
  2.0 0.7 fusion.1
  3.0 0.7 copy-done.3
  3.7 0.7 copy-done.4
  4.4 12.9 %front.1 = (bf16[8,64,1024]{2,1,0:T(8,128)(2,1)}, bf16[8,64,1536]{2,1,0:T(8,128)(2,1)}, bf16[16,72,512]{2,1,0:T(8,128)(2,1)}, bf16[8,64,1024]{2,1,0:T(8,128)(2,1)S(1)}) custom-call(s32[16]{0:T(128)S(1)} %get-tuple-element.16.asker, s32[32]{0:T(128)S(1)} %reshape.65.request, s32[8]{0:T(128)S(1)} %compare_convert_fusion.1.holding, s32[8]{0:T(128)S(1)} %and_select_fusion.held, ...), custom_call_target="tpu_custom_call" | custom-call | flops 4000000000 | bytes 15000000 | tf_op jit(solution)/shard_map/front/pallas_call | solution.py:339
  17.4 7.4 %all-to-all-start = ((bf16[16,72,512]{2,1,0:T(8,128)(2,1)}), bf16[16,72,512]{2,1,0:T(8,128)(2,1)S(1)}, u32[]{:S(2)}, u32[]{:S(2)}) async-start(bf16[16,72,512]{2,1,0:T(8,128)(2,1)} %get-tuple-element.9), calls=%async_computation | async-start | bytes 2359296 | tf_op jit(solution)/shard_map/all_to_all | solution.py:383
  24.8 0.2 dynamic-slice_add_fusion
  25.1 1.5 %collective-permute-start.1 = (bf16[128,1024]{1,0:T(8,128)(2,1)S(1)}, bf16[128,1024]{1,0:T(8,128)(2,1)}, u32[]{:S(2)}, u32[]{:S(2)}) collective-permute-start(bf16[128,1024]{1,0:T(8,128)(2,1)S(1)} %constant_dynamic-slice_fusion.2), channel_id=1, source_target_pairs={{0,2},{1,3},{2,0},{3,1},{4,6},{5,7},{6,4},{7,5},{8,10},{9,11},{10,... | collective-permute-start | bytes 786440 | tf_op jit(solution)/shard_map/ppermute | solution.py:280
  26.5 15.8 %collective-permute-done.1 = bf16[128,1024]{1,0:T(8,128)(2,1)} collective-permute-done((bf16[128,1024]{1,0:T(8,128)(2,1)S(1)}, bf16[128,1024]{1,0:T(8,128)(2,1)}, u32[]{:S(2)}, u32[]{:S(2)}) %collective-permute-start.1) | collective-permute-done | bytes 262176 | tf_op jit(solution)/shard_map/ppermute | solution.py:280
  42.4 1.0 dynamic-slice_add_fusion.1
  43.5 7.2 %collective-permute-done.2 = bf16[64,1024]{1,0:T(8,128)(2,1)S(1)} collective-permute-done((bf16[64,1024]{1,0:T(8,128)(2,1)S(1)}, bf16[64,1024]{1,0:T(8,128)(2,1)S(1)}, u32[]{:S(2)}, u32[]{:S(2)}) %collective-permute-start.2) | collective-permute-done | bytes 131104 | tf_op jit(solution)/shard_map/ppermute | solution.py:280
  50.8 0.1 collective-permute-start.3
  50.9 4.1 %collective-permute-done.3 = bf16[32,1024]{1,0:T(8,128)(2,1)S(1)} collective-permute-done((bf16[32,1024]{1,0:T(8,128)(2,1)S(1)}, bf16[32,1024]{1,0:T(8,128)(2,1)S(1)}, u32[]{:S(2)}, u32[]{:S(2)}) %collective-permute-start.3) | collective-permute-done | bytes 65568 | tf_op jit(solution)/shard_map/ppermute | solution.py:280
  55.1 0.2 collective-permute-start.4
  55.3 4.6 %collective-permute-done.4 = bf16[32,1024]{1,0:T(8,128)(2,1)S(1)} collective-permute-done((bf16[32,1024]{1,0:T(8,128)(2,1)S(1)}, bf16[32,1024]{1,0:T(8,128)(2,1)S(1)}, u32[]{:S(2)}, u32[]{:S(2)}) %collective-permute-start.4) | collective-permute-done | bytes 65568 | tf_op jit(solution)/shard_map/ppermute | solution.py:284
  60.0 6.6 %peer.1 = bf16[16,72,512]{2,1,0:T(8,128)(2,1)} custom-call(s32[32]{0:T(128)S(1)} %reshape.70.asked, bf16[16,72,512]{2,1,0:T(8,128)(2,1)S(1)} %all-to-all-done.received, bf16[8,64,1536]{2,1,0:T(8,128)(2,1)S(1)} %copy-done.6), custom_call_target="tpu_custom_call" | custom-call | flops 2000000000 | bytes 4000000 | tf_op jit(solution)/shard_map/peer/pallas_call | solution.py:388
  66.6 10.1 %all-to-all-start.1 = ((bf16[16,72,512]{2,1,0:T(8,128)(2,1)}), bf16[16,72,512]{2,1,0:T(8,128)(2,1)S(1)}, u32[]{:S(2)}, u32[]{:S(2)}) async-start(bf16[16,72,512]{2,1,0:T(8,128)(2,1)} %peer.1), calls=%async_computation.1 | async-start | bytes 2359296 | tf_op jit(solution)/shard_map/all_to_all | solution.py:407
  76.7 1.5 %collective-permute-start.5 = (bf16[64,1024]{1,0:T(8,128)(2,1)S(1)}, bf16[64,1024]{1,0:T(8,128)(2,1)S(1)}, u32[]{:S(2)}, u32[]{:S(2)}) collective-permute-start(bf16[64,1024]{1,0:T(8,128)(2,1)S(1)} %pad_maximum_fusion.3), channel_id=1, source_target_pairs={{0,4},{1,5},{2,6},{3,7},{4,0},{5,1},{6,2},{7,3},{8,12},{9,13},{10,... | collective-permute-start | bytes 393224 | tf_op jit(solution)/shard_map/ppermute | solution.py:284
  78.2 21.0 %collective-permute-done.5 = bf16[64,1024]{1,0:T(8,128)(2,1)S(1)} collective-permute-done((bf16[64,1024]{1,0:T(8,128)(2,1)S(1)}, bf16[64,1024]{1,0:T(8,128)(2,1)S(1)}, u32[]{:S(2)}, u32[]{:S(2)}) %collective-permute-start.5) | collective-permute-done | bytes 131104 | tf_op jit(solution)/shard_map/ppermute | solution.py:284
  99.2 1.2 collective-permute-start.6
  100.4 0.2 select_reduce_fusion.3
  100.6 6.5 %collective-permute-done.6 = bf16[128,1024]{1,0:T(8,128)(2,1)S(1)} collective-permute-done((bf16[128,1024]{1,0:T(8,128)(2,1)S(1)}, bf16[128,1024]{1,0:T(8,128)(2,1)S(1)}, u32[]{:S(2)}, u32[]{:S(2)}) %collective-permute-start.6) | collective-permute-done | bytes 262176 | tf_op jit(solution)/shard_map/ppermute | solution.py:284
  107.2 1.3 %collective-permute-start.7 = (bf16[256,1024]{1,0:T(8,128)(2,1)S(1)}, bf16[256,1024]{1,0:T(8,128)(2,1)S(1)}, u32[]{:S(2)}, u32[]{:S(2)}) collective-permute-start(bf16[256,1024]{1,0:T(8,128)(2,1)S(1)} %pad_maximum_fusion.1), channel_id=1, source_target_pairs={{0,1},{1,0},{2,3},{3,2},{4,5},{5,4},{6,7},{7,6},{8,9},{9,8},{10,11... | collective-permute-start | bytes 1572872 | tf_op jit(solution)/shard_map/ppermute | solution.py:284
  108.5 0.2 compare_reduce_fusion
  108.7 1.3 %collective-permute-done.7 = bf16[256,1024]{1,0:T(8,128)(2,1)S(1)} collective-permute-done((bf16[256,1024]{1,0:T(8,128)(2,1)S(1)}, bf16[256,1024]{1,0:T(8,128)(2,1)S(1)}, u32[]{:S(2)}, u32[]{:S(2)}) %collective-permute-start.7) | collective-permute-done | bytes 524320 | tf_op jit(solution)/shard_map/ppermute | solution.py:284
  110.0 0.2 broadcast_select_fusion.1
  110.4 1.3 %copy-done.7 = bf16[8,64,1536]{2,1,0:T(8,128)(2,1)S(1)} copy-done((bf16[8,64,1536]{2,1,0:T(8,128)(2,1)S(1)}, bf16[8,64,1536]{2,1,0:T(8,128)(2,1)}, u32[]{:S(2)}) %copy-start.7) | copy-done | bytes 1572888
  111.7 3.0 %own.1 = (f32[8,64,512]{2,1,0:T(8,128)S(1)}, f32[8,64,512]{2,1,0:T(8,128)S(1)}) custom-call(s32[8]{0:T(128)S(1)} %copy-done.5, s32[8]{0:T(128)S(1)} %and_convert_fusion.anchor_ok, bf16[8,64,1536]{2,1,0:T(8,128)(2,1)S(1)} %copy-done.7, bf16[8,64,1024]{2,1,0:T(8,128)(2,1)S(1)} %bitcast.10), custom_call_target="tpu_custom_call" | custom-call | flops 1000000000 | bytes 4000000 | tf_op jit(solution)/shard_map/own/pallas_call | solution.py:409
  114.7 1.0 copy-done.1
  115.7 1.2 copy-done.2
  116.9 6.4 %merge.1 = bf16[8,64,1024]{2,1,0:T(8,128)(2,1)} custom-call(s32[16]{0:T(128)S(1)} %get-tuple-element.16.asker, s32[16]{0:T(128)S(1)} %compare_convert_fusion.has_peer, bf16[16,72,512]{2,1,0:T(8,128)(2,1)S(1)} %all-to-all-done.1.replies, f32[8,64,512]{2,1,0:T(8,128)S(1)} %get-tuple-element.12.own_out, f32[8,64,512]{2,1,0:T(8,128)S(1)} %copy-done.2, ...), custom_call_target="tpu_custom_call" | custom-call | flops 1000000000 | bytes 6000000 | tf_op jit(solution)/shard_map/merge/pallas_call | solution.py:431
  (42 shorter events, 1.1 us)
Async XLA Ops:
  3.0 0.7 copy-start.3
  3.7 0.7 copy-start.4
  17.3 7.5 %collective-permute-start = (bf16[256,1024]{1,0:T(8,128)(2,1)S(1)}, bf16[256,1024]{1,0:T(8,128)(2,1)S(1)}, u32[]{:S(2)}, u32[]{:S(2)}) collective-permute-start(bf16[256,1024]{1,0:T(8,128)(2,1)S(1)} %constant_dynamic-slice_fusion.3), channel_id=1, source_target_pairs={{0,1},{1,0},{2,3},{3,2},{4,5},{5,4},{6,7},{7,6},{8,9},{9,8},{10,11... | collective-permute-start | bytes 1572872 | tf_op jit(solution)/shard_map/ppermute | solution.py:280
  17.4 42.5 %all-to-all-start = ((bf16[16,72,512]{2,1,0:T(8,128)(2,1)}), bf16[16,72,512]{2,1,0:T(8,128)(2,1)S(1)}, u32[]{:S(2)}, u32[]{:S(2)}) async-start(bf16[16,72,512]{2,1,0:T(8,128)(2,1)} %get-tuple-element.9), calls=%async_computation | async-start | bytes 2359296 | tf_op jit(solution)/shard_map/all_to_all | solution.py:383
  25.0 35.0 %copy-start.6 = (bf16[8,64,1536]{2,1,0:T(8,128)(2,1)S(1)}, bf16[8,64,1536]{2,1,0:T(8,128)(2,1)}, u32[]{:S(2)}) copy-start(bf16[8,64,1536]{2,1,0:T(8,128)(2,1)} %get-tuple-element.10.packed) | copy-start | bytes 4718596
  25.1 17.3 %collective-permute-start.1 = (bf16[128,1024]{1,0:T(8,128)(2,1)S(1)}, bf16[128,1024]{1,0:T(8,128)(2,1)}, u32[]{:S(2)}, u32[]{:S(2)}) collective-permute-start(bf16[128,1024]{1,0:T(8,128)(2,1)S(1)} %constant_dynamic-slice_fusion.2), channel_id=1, source_target_pairs={{0,2},{1,3},{2,0},{3,1},{4,6},{5,7},{6,4},{7,5},{8,10},{9,11},{10,... | collective-permute-start | bytes 786440 | tf_op jit(solution)/shard_map/ppermute | solution.py:280
  43.4 7.3 %collective-permute-start.2 = (bf16[64,1024]{1,0:T(8,128)(2,1)S(1)}, bf16[64,1024]{1,0:T(8,128)(2,1)S(1)}, u32[]{:S(2)}, u32[]{:S(2)}) collective-permute-start(bf16[64,1024]{1,0:T(8,128)(2,1)S(1)} %constant_dynamic-slice_fusion.1), channel_id=1, source_target_pairs={{0,4},{1,5},{2,6},{3,7},{4,0},{5,1},{6,2},{7,3},{8,12},{9,13},{10,... | collective-permute-start | bytes 393224 | tf_op jit(solution)/shard_map/ppermute | solution.py:280
  50.8 4.3 %collective-permute-start.3 = (bf16[32,1024]{1,0:T(8,128)(2,1)S(1)}, bf16[32,1024]{1,0:T(8,128)(2,1)S(1)}, u32[]{:S(2)}, u32[]{:S(2)}) collective-permute-start(bf16[32,1024]{1,0:T(8,128)(2,1)S(1)} %constant_dynamic-slice_fusion), channel_id=1, source_target_pairs={{0,8},{1,9},{2,10},{3,11},{4,12},{5,13},{6,14},{7,15},{8,0},{9,1},... | collective-permute-start | bytes 196616 | tf_op jit(solution)/shard_map/ppermute | solution.py:280
  55.1 4.8 %collective-permute-start.4 = (bf16[32,1024]{1,0:T(8,128)(2,1)S(1)}, bf16[32,1024]{1,0:T(8,128)(2,1)S(1)}, u32[]{:S(2)}, u32[]{:S(2)}) collective-permute-start(bf16[32,1024]{1,0:T(8,128)(2,1)S(1)} %dynamic-slice_add_fusion.3), channel_id=1, source_target_pairs={{0,8},{1,9},{2,10},{3,11},{4,12},{5,13},{6,14},{7,15},{8,0},{9,1},... | collective-permute-start | bytes 196616 | tf_op jit(solution)/shard_map/ppermute | solution.py:284
  66.6 33.8 %copy-start.5 = (s32[8]{0:T(128)S(1)}, s32[8]{0:T(128)}, u32[]{:S(2)}) copy-start(s32[8]{0:T(128)} %submap.1) | copy-start | bytes 100
  66.6 33.8 %copy-start.9 = (s32[8]{0:T(128)S(1)}, s32[8]{0:T(128)}, u32[]{:S(2)}) copy-start(s32[8]{0:T(128)} %param.19) | copy-start | bytes 100
  66.6 49.1 %all-to-all-start.1 = ((bf16[16,72,512]{2,1,0:T(8,128)(2,1)}), bf16[16,72,512]{2,1,0:T(8,128)(2,1)S(1)}, u32[]{:S(2)}, u32[]{:S(2)}) async-start(bf16[16,72,512]{2,1,0:T(8,128)(2,1)} %peer.1), calls=%async_computation.1 | async-start | bytes 2359296 | tf_op jit(solution)/shard_map/all_to_all | solution.py:407
  76.7 22.5 %collective-permute-start.5 = (bf16[64,1024]{1,0:T(8,128)(2,1)S(1)}, bf16[64,1024]{1,0:T(8,128)(2,1)S(1)}, u32[]{:S(2)}, u32[]{:S(2)}) collective-permute-start(bf16[64,1024]{1,0:T(8,128)(2,1)S(1)} %pad_maximum_fusion.3), channel_id=1, source_target_pairs={{0,4},{1,5},{2,6},{3,7},{4,0},{5,1},{6,2},{7,3},{8,12},{9,13},{10,... | collective-permute-start | bytes 393224 | tf_op jit(solution)/shard_map/ppermute | solution.py:284
  78.2 30.3 %copy-start.8 = (s32[8,16]{1,0:T(8,128)S(1)}, s32[8,16]{1,0:T(8,128)}, u32[]{:S(2)}) copy-start(s32[8,16]{1,0:T(8,128)} %param.17) | copy-start | bytes 1540
  99.2 7.8 %collective-permute-start.6 = (bf16[128,1024]{1,0:T(8,128)(2,1)S(1)}, bf16[128,1024]{1,0:T(8,128)(2,1)S(1)}, u32[]{:S(2)}, u32[]{:S(2)}) collective-permute-start(bf16[128,1024]{1,0:T(8,128)(2,1)S(1)} %pad_maximum_fusion.2), channel_id=1, source_target_pairs={{0,2},{1,3},{2,0},{3,1},{4,6},{5,7},{6,4},{7,5},{8,10},{9,11},{10,... | collective-permute-start | bytes 786440 | tf_op jit(solution)/shard_map/ppermute | solution.py:284
  107.2 2.8 %collective-permute-start.7 = (bf16[256,1024]{1,0:T(8,128)(2,1)S(1)}, bf16[256,1024]{1,0:T(8,128)(2,1)S(1)}, u32[]{:S(2)}, u32[]{:S(2)}) collective-permute-start(bf16[256,1024]{1,0:T(8,128)(2,1)S(1)} %pad_maximum_fusion.1), channel_id=1, source_target_pairs={{0,1},{1,0},{2,3},{3,2},{4,5},{5,4},{6,7},{7,6},{8,9},{9,8},{10,11... | collective-permute-start | bytes 1572872 | tf_op jit(solution)/shard_map/ppermute | solution.py:284
  110.3 1.4 %copy-start.7 = (bf16[8,64,1536]{2,1,0:T(8,128)(2,1)S(1)}, bf16[8,64,1536]{2,1,0:T(8,128)(2,1)}, u32[]{:S(2)}) copy-start(bf16[8,64,1536]{2,1,0:T(8,128)(2,1)} %get-tuple-element.10.packed) | copy-start | bytes 4718596
  111.7 4.0 %copy-start = (bf16[512,1024]{1,0:T(8,128)(2,1)S(1)}, bf16[512,1024]{1,0:T(8,128)(2,1)}, u32[]{:S(2)}) copy-start(bf16[512,1024]{1,0:T(8,128)(2,1)} %out_global.1) | copy-start | bytes 3145732
  114.7 1.0 copy-start.1
  115.7 1.2 copy-start.2

commit v2 on v1

--- a/solution.py
+++ b/solution.py
@@ -12,8 +12,8 @@
 CAP_K = 2
 GROUP = 4
 WIDE = GROUP * HD
-EXTRA = 8
-ANCHOR = "butterfly"
+PIECE = 16
+MESH = pl.DeviceIdType.MESH
 
 masked_score = -1e30
 
@@ -67,6 +67,7 @@
     frame_out,
     packed,
     message,
+    notes,
     anchors,
 ):
     step = pl.program_id(0)
@@ -106,24 +107,30 @@
 
     @pl.when(step == pl.num_programs(0) - 1)
     def _():
-        row = lax.broadcasted_iota(jnp.int32, (EXTRA, inner), 0)
-        lane = lax.broadcasted_iota(jnp.int32, (EXTRA, inner), 1)
+        row = lax.broadcasted_iota(jnp.int32, notes.shape[1:], 0)
+        lane = lax.broadcasted_iota(jnp.int32, notes.shape[1:], 1)
+        frame_of_key = (row * lane.shape[1] + lane) // length
 
         def put(b, carry):
-            message[b, :length] = packed[asker[b], :, :inner]
-            note = jnp.where(lane == 0, request[2 * b], jnp.where(lane == 1, request[2 * b + 1], 0))
-            note = jnp.where(row == 0, note, 0)
-            message[b, length:] = note.astype(jnp.float32).astype(jnp.bfloat16)
+            message[b] = packed[asker[b], :, :inner]
+            wanted = (frame_of_key == request[2 * b]) | (frame_of_key == request[2 * b + 1])
+            notes[b] = jnp.where(wanted, 1.0, 0.0)
             return carry
 
         lax.fori_loop(0, message.shape[0], put, 0)
+        count = length // PIECE
 
         def hold(s, carry):
             taken = packed[held[s], :, inner:]
-            anchors[s] = jnp.where(holding[s] > 0, taken, jnp.zeros_like(taken))
+            taken = jnp.where(holding[s] > 0, taken, jnp.zeros_like(taken))
+            for r in range(count):
+                for c in range(2):
+                    anchors[(s * count + r) * 2 + c] = taken[
+                        r * PIECE : (r + 1) * PIECE, c * inner : (c + 1) * inner
+                    ]
             return carry
 
-        lax.fori_loop(0, anchors.shape[0], hold, 0)
+        lax.fori_loop(0, held.shape[0], hold, 0)
 
 
 def split_three(values):
@@ -134,44 +141,163 @@
     return high, middle, low
 
 
-def peer_kernel(asked, received, packed, reply):
-    step = pl.program_id(0)
-    per_step = received.shape[0]
-    length = packed.shape[1]
+def exchange_kernel(
+    n,
+    queries,
+    notes,
+    packed,
+    anchors,
+    replies,
+    stats,
+    table,
+    queries_in,
+    notes_in,
+    reply,
+    stat,
+    arrived,
+    work,
+    query_sent,
+    query_got,
+    note_sent,
+    note_got,
+    reply_sent,
+    reply_got,
+    stat_sent,
+    stat_got,
+    anchor_sent,
+    anchor_got,
+):
+    me = lax.axis_index("frames")
+    frames, length, _ = packed.shape
     inner = HEADS * HD
+    keys_in_all = frames * length
+
+    def copy(source, target, sent, got, device):
+        return pltpu.make_async_remote_copy(
+            src_ref=source,
+            dst_ref=target,
+            send_sem=sent,
+            recv_sem=got,
+            device_id={"frames": device},
+            device_id_type=MESH,
+        )
+
+    def query_copies(k):
+        peer = lax.rem(me + k, n)
+        return (
+            copy(queries.at[peer], queries_in.at[me], query_sent.at[k], query_got.at[k], peer),
+            copy(notes.at[peer], notes_in.at[me], note_sent.at[k], note_got.at[k], peer),
+        )
+
+    def reply_copies(k):
+        peer = lax.rem(me - k + n, n)
+        return (
+            copy(reply.at[k], replies.at[me], reply_sent.at[k], reply_got.at[k], peer),
+            copy(stat.at[k], stats.at[me], stat_sent.at[k], stat_got.at[k], peer),
+        )
+
+    barrier = pltpu.get_barrier_semaphore()
+
+    def greet(k, carry):
+        pl.semaphore_signal(
+            barrier, inc=1, device_id={"frames": lax.rem(me + k, n)}, device_id_type=MESH
+        )
+        return carry
+
+    lax.fori_loop(1, n, greet, 0)
+    work[...] = anchors[...]
+    replies[me] = jnp.zeros(replies.shape[1:], replies.dtype)
+    stats[me] = jnp.zeros(stats.shape[1:], stats.dtype)
+    pl.semaphore_wait(barrier, n - 1)
+
+    stages = n.bit_length() - 1
+    pieces = table.shape[0]
+
+    def ask(k, carry):
+        for c in query_copies(k):
+            c.start()
+        return carry
+
+    base = me * 0
+    size = pieces
+    bounds = [1 + (n - 1) * i // stages for i in range(stages + 1)]
+    for i in range(stages):
+        half = size // 2
+        bit = (me // 2**i) % 2
+        partner = me + 2**i * (1 - 2 * bit)
+        mine = base + bit * half
+        other = base + (1 - bit) * half
+        start = pieces - size
+        moving = copy(
+            work.at[pl.ds(other, half)],
+            arrived.at[pl.ds(start, half)],
+            anchor_sent.at[i],
+            anchor_got.at[i],
+            partner,
+        )
+        moving.start()
+        lax.fori_loop(bounds[i], bounds[i + 1], ask, 0)
+        moving.wait()
+        work[pl.ds(mine, half)] = work[pl.ds(mine, half)] + arrived[pl.ds(start, half)]
+        base, size = mine, half
+    table[pl.ds(base, size)] = work[pl.ds(base, size)]
+
     masks = head_masks(length)
     rows = GROUP * length
-    second_half = lax.broadcasted_iota(jnp.int32, (1, 2 * length), 1) >= length
     eye = lax.broadcasted_iota(jnp.int32, (rows, rows), 0) == lax.broadcasted_iota(
         jnp.int32, (rows, rows), 1
     )
-    note_row = lax.broadcasted_iota(jnp.int32, (EXTRA, rows), 0)
-    for i in range(per_step):
-        b = step * per_step + i
-        one, two = asked[2 * b], asked[2 * b + 1]
-        visible = jnp.where(second_half, two, one) >= 0
-        one, two = jnp.maximum(one, 0), jnp.maximum(two, 0)
+
+    def answer(k, carry):
+        source = lax.rem(me - k + n, n)
+        for c in query_copies(k):
+            c.wait_recv()
+        note = notes_in[source]
+        lines = keys_in_all // note.shape[1]
+        visible = jnp.concatenate([note[j : j + 1] for j in range(lines)], axis=1) > 0.5
+        pieces_out = []
         for g in range(HEADS // GROUP):
             low = g * WIDE
-            keys = jnp.concatenate(
-                [packed[f, :, inner + low : inner + low + WIDE] for f in (one, two)], axis=0
-            )
-            values = jnp.concatenate(
-                [packed[f, :, 2 * inner + low : 2 * inner + low + WIDE] for f in (one, two)],
-                axis=0,
+            keys = packed[:, :, inner + low : inner + low + WIDE].reshape(keys_in_all, WIDE)
+            values = packed[:, :, 2 * inner + low : 2 * inner + low + WIDE].reshape(
+                keys_in_all, WIDE
             )
             out, lse = attend_group(
-                received[i, :length, low : low + WIDE], keys, values, masks, visible
+                queries_in[source, :, low : low + WIDE], keys, values, masks, visible
             )
-            reply[i, :length, low : low + WIDE] = out.astype(jnp.bfloat16)
+            reply[k, :, low : low + WIDE] = out.astype(jnp.bfloat16)
             line = jnp.sum(jnp.where(eye, lse, 0.0), axis=0, keepdims=True)
-            high, middle, small = [p.astype(jnp.float32) for p in split_three(line)]
-            note = jnp.where(
-                note_row == 0,
-                high,
-                jnp.where(note_row == 1, middle, jnp.where(note_row == 2, small, 0.0)),
-            )
-            reply[i, length:, low : low + WIDE] = note.astype(jnp.bfloat16)
+            width = note.shape[1]
+            pieces_out += [line[:, j * width : (j + 1) * width] for j in range(rows // width)]
+        spare = jnp.zeros((note.shape[0] - len(pieces_out), note.shape[1]), jnp.float32)
+        stat[k] = jnp.concatenate(pieces_out + [spare], axis=0)
+        for c in reply_copies(k):
+            c.start()
+        return carry
+
+    for i in reversed(range(stages)):
+        bit = (me // 2**i) % 2
+        partner = me + 2**i * (1 - 2 * bit)
+        moving = copy(
+            table.at[pl.ds(base, size)],
+            table.at[pl.ds(base, size)],
+            anchor_sent.at[stages + i],
+            anchor_got.at[stages + i],
+            partner,
+        )
+        moving.start()
+        lax.fori_loop(bounds[stages - 1 - i], bounds[stages - i], answer, 0)
+        moving.wait()
+        base, size = base - bit * size, 2 * size
+
+    def finish(k, carry):
+        for c in query_copies(k):
+            c.wait_send()
+        for c in reply_copies(k):
+            c.wait()
+        return carry
+
+    lax.fori_loop(1, n, finish, 0)
 
 
 def own_kernel(submap, anchor_ok, packed, table, out_ref, top_ref):
@@ -187,13 +313,13 @@
         for g in range(HEADS // GROUP):
             low = g * WIDE
             keys = jnp.concatenate(
-                [packed[f, :, inner + low : inner + low + WIDE], table[s, :, low : low + WIDE]],
+                [packed[f, :, inner + low : inner + low + WIDE], table[s, :, 0, :, low : low + WIDE].reshape(length, WIDE)],
                 axis=0,
             )
             values = jnp.concatenate(
                 [
                     packed[f, :, 2 * inner + low : 2 * inner + low + WIDE],
-                    table[s, :, inner + low : inner + low + WIDE],
+                    table[s, :, 1, :, low : low + WIDE].reshape(length, WIDE),
                 ],
                 axis=0,
             )
@@ -207,7 +333,7 @@
             top_ref[i, :, low : low + WIDE] = spread
 
 
-def merge_kernel(asker, has_peer, replies, own_out, own_top, out_global, update, acc, top, total):
+def merge_kernel(asker, has_peer, replies, stats, own_out, own_top, out_global, update, acc, top, total):
     frames, length, inner = own_out.shape
     acc[...] = own_out[...]
     top[...] = own_top[...]
@@ -227,11 +353,16 @@
             f = asker[b]
             for g in range(HEADS // GROUP):
                 cols = slice(g * WIDE, (g + 1) * WIDE)
-                notes = replies[b, length:, cols].astype(jnp.float32)
+                lines = stats[b]
+                count = rows // lines.shape[1]
+                line = jnp.concatenate(
+                    [lines[j : j + 1] for j in range(g * count, (g + 1) * count)], axis=1
+                )
+                notes = split_three(line)
                 stacked = jnp.concatenate(
                     [
-                        jnp.where(place, notes[k : k + 1], 0.0).astype(jnp.bfloat16)
-                        for k in range(3)
+                        jnp.where(place, part.astype(jnp.float32), 0.0).astype(jnp.bfloat16)
+                        for part in notes
                     ],
                     axis=0,
                 )
@@ -243,7 +374,7 @@
                 top[f, :, cols] = largest
                 total[f, :, cols] = total[f, :, cols] * keep + new
                 acc[f, :, cols] = acc[f, :, cols] * keep + (
-                    replies[b, :length, cols].astype(jnp.float32) * new
+                    replies[b, :, cols].astype(jnp.float32) * new
                 )
 
         return carry
@@ -259,33 +390,6 @@
 
 def whole(shape):
     return pl.BlockSpec(shape, lambda *_: (0,) * len(shape))
-
-
-def share_anchors(terms, position, block_count):
-    if ANCHOR == "psum":
-        return lax.psum(terms, "frames")
-    shape = terms.shape
-    held = terms.reshape(shape[0] * shape[1], shape[2])
-    if ANCHOR == "a2a":
-        pieces = held.reshape(block_count, -1, shape[2])
-        got = lax.all_to_all(pieces, "frames", split_axis=0, concat_axis=0, tiled=True)
-        mine = jnp.sum(got.astype(jnp.float32), axis=0).astype(jnp.bfloat16)
-        return lax.all_gather(mine, "frames", tiled=True).reshape(shape)
-    bits = block_count.bit_length() - 1
-    for bit in range(bits):
-        half = held.shape[0] // 2
-        mine = (position >> bit) & 1
-        keep = lax.dynamic_slice_in_dim(held, mine * half, half, 0)
-        send = lax.dynamic_slice_in_dim(held, (1 - mine) * half, half, 0)
-        got = lax.ppermute(send, "frames", [(d, d ^ (1 << bit)) for d in range(block_count)])
-        held = keep + got
-    for bit in reversed(range(bits)):
-        mine = (position >> bit) & 1
-        got = lax.ppermute(held, "frames", [(d, d ^ (1 << bit)) for d in range(block_count)])
-        held = jnp.concatenate(
-            [jnp.where(mine == 0, held, got), jnp.where(mine == 0, got, held)], axis=0
-        )
-    return held.reshape(shape)
 
 
 def local(
@@ -333,10 +437,13 @@
     holding = (submap_anchor // frame_count == position).astype(jnp.int32)
     held = submap_anchor % frame_count
 
-    rows = token_count + EXTRA
+    note_shape = (block_count, 8, 128)
+    piece_count = submap_count * token_count // PIECE * 2
+    pieces = (piece_count, PIECE, inner_width)
+    assert frame_count * token_count <= 1024 and piece_count % block_count == 0
     steps = 2
     each = frame_count // steps
-    frame_out, packed, message, anchor_terms = pl.pallas_call(
+    frame_out, packed, message, notes, anchor_terms = pl.pallas_call(
         front_kernel,
         grid_spec=pltpu.PrefetchScalarGridSpec(
             num_scalar_prefetch=4,
@@ -352,15 +459,17 @@
             out_specs=[
                 pl.BlockSpec((each, token_count, feature_count), lambda i, *_: (i, 0, 0)),
                 whole((frame_count, token_count, 3 * inner_width)),
-                whole((block_count, rows, inner_width)),
-                whole((submap_count, token_count, 2 * inner_width)),
+                whole((block_count, token_count, inner_width)),
+                whole(note_shape),
+                whole(pieces),
             ],
         ),
         out_shape=[
             jax.ShapeDtypeStruct(tokens.shape, jnp.bfloat16),
             jax.ShapeDtypeStruct((frame_count, token_count, 3 * inner_width), jnp.bfloat16),
-            jax.ShapeDtypeStruct((block_count, rows, inner_width), jnp.bfloat16),
-            jax.ShapeDtypeStruct((submap_count, token_count, 2 * inner_width), jnp.bfloat16),
+            jax.ShapeDtypeStruct((block_count, token_count, inner_width), jnp.bfloat16),
+            jax.ShapeDtypeStruct(note_shape, jnp.float32),
+            jax.ShapeDtypeStruct(pieces, jnp.bfloat16),
         ],
         compiler_params=pltpu.CompilerParams(vmem_limit_bytes=52 * 2**20),
         cost_estimate=pl.CostEstimate(
@@ -380,31 +489,37 @@
         qkv_global,
     )
 
-    received = lax.all_to_all(message, "frames", split_axis=0, concat_axis=0, tiled=True)
-    table = share_anchors(anchor_terms, position, block_count)
-
-    asked = received[:, token_count, :CAP_K].astype(jnp.int32).reshape(-1)
-    per_step = 4
-    reply = pl.pallas_call(
-        peer_kernel,
-        grid_spec=pltpu.PrefetchScalarGridSpec(
-            num_scalar_prefetch=1,
-            grid=(block_count // per_step,),
-            in_specs=[
-                pl.BlockSpec((per_step, rows, inner_width), lambda i, *_: (i, 0, 0)),
-                whole(packed.shape),
-            ],
-            out_specs=pl.BlockSpec((per_step, rows, inner_width), lambda i, *_: (i, 0, 0)),
-        ),
-        out_shape=jax.ShapeDtypeStruct((block_count, rows, inner_width), jnp.bfloat16),
-        compiler_params=pltpu.CompilerParams(vmem_limit_bytes=24 * 2**20),
+    stages = block_count.bit_length() - 1
+    in_vmem = pl.BlockSpec(memory_space=pltpu.VMEM)
+    per_peer = pltpu.SemaphoreType.DMA((block_count,))
+    replies, stats, table = pl.pallas_call(
+        functools.partial(exchange_kernel, block_count),
+        in_specs=[in_vmem] * 4,
+        out_specs=[in_vmem] * 3,
+        out_shape=[
+            jax.ShapeDtypeStruct(message.shape, jnp.bfloat16),
+            jax.ShapeDtypeStruct(note_shape, jnp.float32),
+            jax.ShapeDtypeStruct(pieces, jnp.bfloat16),
+        ],
+        scratch_shapes=[
+            pltpu.VMEM(message.shape, jnp.bfloat16),
+            pltpu.VMEM(note_shape, jnp.float32),
+            pltpu.VMEM(message.shape, jnp.bfloat16),
+            pltpu.VMEM(note_shape, jnp.float32),
+            pltpu.VMEM(pieces, jnp.bfloat16),
+            pltpu.VMEM(pieces, jnp.bfloat16),
+        ]
+        + [per_peer] * 8
+        + [pltpu.SemaphoreType.DMA((2 * stages,))] * 2,
+        compiler_params=pltpu.CompilerParams(
+            collective_id=0, has_side_effects=True, vmem_limit_bytes=44 * 2**20
+        ),
         cost_estimate=pl.CostEstimate(
-            flops=2 * 10**9, bytes_accessed=4 * 10**6, transcendentals=10**6
-        ),
-        name="peer",
-    )(asked, received, packed)
-
-    replies = lax.all_to_all(reply, "frames", split_axis=0, concat_axis=0, tiled=True)
+            flops=4 * 10**9, bytes_accessed=8 * 10**6, transcendentals=4 * 10**6
+        ),
+        name="exchange",
+    )(message, notes, packed, anchor_terms)
+    table = table.reshape(submap_count, token_count // PIECE, 2, PIECE, inner_width)
 
     own_out, own_top = pl.pallas_call(
         own_kernel,
@@ -435,6 +550,7 @@
             grid=(1,),
             in_specs=[
                 whole(replies.shape),
+                whole(stats.shape),
                 whole(own_out.shape),
                 whole(own_top.shape),
                 whole(out_global.shape),
@@ -448,7 +564,7 @@
             flops=10**9, bytes_accessed=6 * 10**6, transcendentals=10**6
         ),
         name="merge",
-    )(asker_index, has_peer, replies, own_out, own_top, out_global)
+    )(asker_index, has_peer, replies, stats, own_out, own_top, out_global)
     return frame_out, global_update
 
 

time: 125 us -> 108 us (0.86)
  Pallas kernels: 28.8 us -> 97 us
  waiting for transfers between devices: 60.5 us -> 0 us
  starting transfers between devices: 23.4 us -> 0 us
    pallas_call x1, Pallas kernels: 6.55 us -> 74.7 us  [local(): pl.pallas_call(functools.partial(exchange_kernel, block_count), in_specs=...]
    ppermute x8 -> x0, waiting for transfers between devices: 60.5 us -> none  [the longest x4 33.3 us: share_anchors(): lax.ppermute(held, 'frames', [(d, d ^ 1 << bit) for d in range(block_coun...]
    all_to_all x2 -> x0, starting transfers between devices: 17.5 us -> none  [the longest x1 10.1 us: local(): lax.all_to_all(reply, 'frames', split_axis=0, concat_axis=0, tiled=True)]
    ppermute x8 -> x0, starting transfers between devices: 5.9 us -> none  [the longest x4 4.13 us: share_anchors(): lax.ppermute(held, 'frames', [(d, d ^ 1 << bit) for d in range(block_coun...]
    add x4 -> x0, other arithmetic: 1.29 us -> none  [share_anchors(): held = keep + got]
    unnamed x20 -> x14, local copies, waits for them, and re-layouts: 4.9 us -> 4.02 us
  transfers between devices with their start and end apart: 10 -> 0, of which waited for: 7 -> 0; matrix products, arithmetic and copies ran while one was open for 2% -> 0% of each run, Pallas kernels for 2% -> 0%
where the time goes in v2:
time: 108 us; the launch traced here: 106 us
  Pallas kernels  97 us (90%)
  local copies, waits for them, and re-layouts  4.19 us (4%)
  other arithmetic  3.89 us (4%)
    pallas_call x1, Pallas kernels, local(): pl.pallas_call(functools.partial(exchange_kernel, block_count), in_specs=...  74.7 us
    pallas_call x1, Pallas kernels, local(): pl.pallas_call(front_kernel, grid_spec=pltpu.PrefetchScalarGridSpec(num_s...  12.8 us
    pallas_call x1, Pallas kernels, local(): pl.pallas_call(merge_kernel, grid_spec=pltpu.PrefetchScalarGridSpec(num_s...  6.49 us
    unnamed x14, local copies, waits for them, and re-layouts  4.02 us
    pallas_call x1, Pallas kernels, local(): pl.pallas_call(own_kernel, grid_spec=pltpu.PrefetchScalarGridSpec(num_sca...  2.96 us

profile of v2, /device:TPU:1, one launch (start us, length us, event | category | flops | bytes accessed | tf_op | source)
XLA Modules:
  0.0 105.8 jit_solution(7410997951344739082)
XLA Ops:
  0.6 0.7 compare_convert_fusion.1.holding
  1.3 0.9 select_reduce_fusion.3
  2.2 0.9 compare_reduce_fusion
  3.0 0.7 and_select_fusion.held
  3.7 0.7 fusion
  4.4 0.1 select_reduce_fusion.1
  4.6 0.1 copy.14
  4.6 0.1 reshape.58.request
  4.7 0.0 copy-start.1
  4.7 0.7 copy-done.1
  5.4 0.0 copy-start.2
  5.4 0.7 copy-done.2
  6.1 12.8 %front.1 = (bf16[8,64,1024]{2,1,0:T(8,128)(2,1)}, bf16[8,64,1536]{2,1,0:T(8,128)(2,1)}, bf16[16,64,512]{2,1,0:T(8,128)(2,1)S(1)}, f32[16,8,128]{2,1,0:T(8,128)S(1)}, bf16[64,16,512]{2,1,0:T(8,128)(2,1)}) custom-call(s32[16]{0:T(128)S(1)} %get-tuple-element.24.asker, s32[32]{0:T(128)S(1)} %reshape.58.request, s32[8]{0:T(128)S(1)} %compare_convert_fusion.1.holding, ...), custom_call_target="tpu_custom_call" | custom-call | flops 4000000000 | bytes 15000000 | tf_op jit(solution)/shard_map/front/pallas_call | solution.py:446
  18.9 0.0 copy-start.4
  18.9 1.4 %copy-done.4 = bf16[8,64,1536]{2,1,0:T(8,128)(2,1)S(1)} copy-done((bf16[8,64,1536]{2,1,0:T(8,128)(2,1)S(1)}, bf16[8,64,1536]{2,1,0:T(8,128)(2,1)}, u32[]{:S(2)}) %copy-start.4) | copy-done | bytes 1572888
  20.3 0.0 copy-start.6
  20.3 1.2 %copy-done.6 = bf16[64,16,512]{2,1,0:T(8,128)(2,1)S(1)} copy-done((bf16[64,16,512]{2,1,0:T(8,128)(2,1)S(1)}, bf16[64,16,512]{2,1,0:T(8,128)(2,1)}, u32[]{:S(2)}) %copy-start.6) | copy-done | bytes 1048600
  21.6 0.0 copy-start.3
  21.6 0.0 copy-start.5
  21.6 74.7 %exchange.1 = (bf16[16,64,512]{2,1,0:T(8,128)(2,1)S(1)}, f32[16,8,128]{2,1,0:T(8,128)S(1)}, bf16[64,16,512]{2,1,0:T(8,128)(2,1)S(1)}) custom-call(bf16[16,64,512]{2,1,0:T(8,128)(2,1)S(1)} %get-tuple-element.13.queries, f32[16,8,128]{2,1,0:T(8,128)S(1)} %get-tuple-element.14.notes, bf16[8,64,1536]{2,1,0:T(8,128)(2,1)S(1)} %copy-done.4, ...), custom_call_target="tpu_custom_call" | custom-call | flops 4000000000 | bytes 8000000 | tf_op jit(solution)/shard_map/exchange/pallas_call | solution.py:495
  96.3 0.0 copy-start
  96.3 0.0 copy-done.3
  96.3 0.0 copy-done.5
  96.3 3.0 %own.1 = (f32[8,64,512]{2,1,0:T(8,128)S(1)}, f32[8,64,512]{2,1,0:T(8,128)S(1)}) custom-call(s32[8]{0:T(128)S(1)} %copy-done.3, s32[8]{0:T(128)S(1)} %and_convert_fusion.anchor_ok, bf16[8,64,1536]{2,1,0:T(8,128)(2,1)S(1)} %copy-done.5, bf16[8,4,2,16,512]{4,3,2,1,0:T(8,128)(2,1)S(1)} %bitcast.11), custom_call_target="tpu_custom_call" | custom-call | flops 1000000000 | bytes 4000000 | tf_op jit(solution)/shard_map/own/pallas_call | solution.py:524
  99.3 0.0 copy-done
  99.3 6.5 %merge.1 = bf16[8,64,1024]{2,1,0:T(8,128)(2,1)} custom-call(s32[16]{0:T(128)S(1)} %get-tuple-element.24.asker, s32[16]{0:T(128)S(1)} %compare_convert_fusion.has_peer, bf16[16,64,512]{2,1,0:T(8,128)(2,1)S(1)} %get-tuple-element.17.replies, f32[16,8,128]{2,1,0:T(8,128)S(1)} %get-tuple-element.18.stats, f32[8,64,512]{2,1,0:T(8,128)S(1)} %get-tuple-element.20.own_out, ...), custom_call_target="tpu_custom_call" | custom-call | flops 1000000000 | bytes 6000000 | tf_op jit(solution)/shard_map/merge/pallas_call | solution.py:546
  (4 shorter events, 0.0 us)
Async XLA Ops:
  4.7 0.7 copy-start.1
  5.4 0.7 copy-start.2
  18.9 1.4 %copy-start.4 = (bf16[8,64,1536]{2,1,0:T(8,128)(2,1)S(1)}, bf16[8,64,1536]{2,1,0:T(8,128)(2,1)}, u32[]{:S(2)}) copy-start(bf16[8,64,1536]{2,1,0:T(8,128)(2,1)} %get-tuple-element.15.packed) | copy-start | bytes 4718596
  20.3 1.2 %copy-start.6 = (bf16[64,16,512]{2,1,0:T(8,128)(2,1)S(1)}, bf16[64,16,512]{2,1,0:T(8,128)(2,1)}, u32[]{:S(2)}) copy-start(bf16[64,16,512]{2,1,0:T(8,128)(2,1)} %get-tuple-element.16.anchors) | copy-start | bytes 3145732
  21.6 74.7 %copy-start.3 = (s32[8]{0:T(128)S(1)}, s32[8]{0:T(128)}, u32[]{:S(2)}) copy-start(s32[8]{0:T(128)} %submap.1) | copy-start | bytes 100
  21.6 74.7 %copy-start.5 = (bf16[8,64,1536]{2,1,0:T(8,128)(2,1)S(1)}, bf16[8,64,1536]{2,1,0:T(8,128)(2,1)}, u32[]{:S(2)}) copy-start(bf16[8,64,1536]{2,1,0:T(8,128)(2,1)} %get-tuple-element.15.packed) | copy-start | bytes 4718596
  96.3 3.0 %copy-start = (bf16[512,1024]{1,0:T(8,128)(2,1)S(1)}, bf16[512,1024]{1,0:T(8,128)(2,1)}, u32[]{:S(2)}) copy-start(bf16[512,1024]{1,0:T(8,128)(2,1)} %out_global.1) | copy-start | bytes 3145732

commit v3 on v2

--- a/solution.py
+++ b/solution.py
@@ -182,15 +182,19 @@
             device_id_type=MESH,
         )
 
+    def offset(j):
+        odd = (j - 1) % 2
+        return n // 2 + (1 - odd) * ((j - 1) // 2) - odd * (j // 2)
+
     def query_copies(k):
-        peer = lax.rem(me + k, n)
+        peer = lax.rem(me + offset(k), n)
         return (
             copy(queries.at[peer], queries_in.at[me], query_sent.at[k], query_got.at[k], peer),
             copy(notes.at[peer], notes_in.at[me], note_sent.at[k], note_got.at[k], peer),
         )
 
     def reply_copies(k):
-        peer = lax.rem(me - k + n, n)
+        peer = lax.rem(me - offset(k) + n, n)
         return (
             copy(reply.at[k], replies.at[me], reply_sent.at[k], reply_got.at[k], peer),
             copy(stat.at[k], stats.at[me], stat_sent.at[k], stat_got.at[k], peer),
@@ -221,6 +225,8 @@
     base = me * 0
     size = pieces
     bounds = [1 + (n - 1) * i // stages for i in range(stages + 1)]
+    later = max(stages - 1, 1)
+    asks = [1] + [1 + n // 2 + (n // 2 - 1) * i // later for i in range(stages)]
     for i in range(stages):
         half = size // 2
         bit = (me // 2**i) % 2
@@ -236,7 +242,7 @@
             partner,
         )
         moving.start()
-        lax.fori_loop(bounds[i], bounds[i + 1], ask, 0)
+        lax.fori_loop(asks[i], asks[i + 1], ask, 0)
         moving.wait()
         work[pl.ds(mine, half)] = work[pl.ds(mine, half)] + arrived[pl.ds(start, half)]
         base, size = mine, half
@@ -249,7 +255,7 @@
     )
 
     def answer(k, carry):
-        source = lax.rem(me - k + n, n)
+        source = lax.rem(me - offset(k) + n, n)
         for c in query_copies(k):
             c.wait_recv()
         note = notes_in[source]
@@ -300,14 +306,13 @@
     lax.fori_loop(1, n, finish, 0)
 
 
-def own_kernel(submap, anchor_ok, packed, table, out_ref, top_ref):
-    step = pl.program_id(0)
+def attend_own(submap, anchor_ok, packed, table, out_ref, top_ref):
     frames, length, _ = out_ref.shape
     inner = HEADS * HD
     masks = head_masks(length)
     second_half = lax.broadcasted_iota(jnp.int32, (1, 2 * length), 1) >= length
     for i in range(frames):
-        f = step * frames + i
+        f = i
         s = submap[f]
         visible = jnp.where(second_half, anchor_ok[f], 1) > 0
         for g in range(HEADS // GROUP):
@@ -333,10 +338,23 @@
             top_ref[i, :, low : low + WIDE] = spread
 
 
-def merge_kernel(asker, has_peer, replies, stats, own_out, own_top, out_global, update, acc, top, total):
-    frames, length, inner = own_out.shape
-    acc[...] = own_out[...]
-    top[...] = own_top[...]
+def merge_kernel(
+    asker,
+    has_peer,
+    submap,
+    anchor_ok,
+    replies,
+    stats,
+    packed,
+    table,
+    out_global,
+    update,
+    acc,
+    top,
+    total,
+):
+    frames, length, inner = acc.shape
+    attend_own(submap, anchor_ok, packed, table, acc, top)
     total[...] = jnp.ones_like(total)
     rows = GROUP * length
     query_of = lax.broadcasted_iota(jnp.int32, (length, rows), 1) % length
@@ -521,42 +539,21 @@
     )(message, notes, packed, anchor_terms)
     table = table.reshape(submap_count, token_count // PIECE, 2, PIECE, inner_width)
 
-    own_out, own_top = pl.pallas_call(
-        own_kernel,
-        grid_spec=pltpu.PrefetchScalarGridSpec(
-            num_scalar_prefetch=2,
-            grid=(steps,),
-            in_specs=[whole(packed.shape), whole(table.shape)],
-            out_specs=[
-                pl.BlockSpec((each, token_count, inner_width), lambda i, *_: (i, 0, 0)),
-                pl.BlockSpec((each, token_count, inner_width), lambda i, *_: (i, 0, 0)),
-            ],
-        ),
-        out_shape=[
-            jax.ShapeDtypeStruct((frame_count, token_count, inner_width), jnp.float32),
-            jax.ShapeDtypeStruct((frame_count, token_count, inner_width), jnp.float32),
-        ],
-        compiler_params=pltpu.CompilerParams(vmem_limit_bytes=24 * 2**20),
-        cost_estimate=pl.CostEstimate(
-            flops=10**9, bytes_accessed=4 * 10**6, transcendentals=10**6
-        ),
-        name="own",
-    )(submap_ids, anchor_ok, packed, table)
-
     global_update = pl.pallas_call(
         merge_kernel,
         grid_spec=pltpu.PrefetchScalarGridSpec(
-            num_scalar_prefetch=2,
+            num_scalar_prefetch=4,
             grid=(1,),
             in_specs=[
                 whole(replies.shape),
                 whole(stats.shape),
-                whole(own_out.shape),
-                whole(own_top.shape),
+                whole(packed.shape),
+                whole(table.shape),
                 whole(out_global.shape),
             ],
             out_specs=whole(tokens.shape),
-            scratch_shapes=[pltpu.VMEM(own_out.shape, jnp.float32)] * 3,
+            scratch_shapes=[pltpu.VMEM((frame_count, token_count, inner_width), jnp.float32)]
+            * 3,
         ),
         out_shape=jax.ShapeDtypeStruct(tokens.shape, jnp.bfloat16),
         compiler_params=pltpu.CompilerParams(vmem_limit_bytes=40 * 2**20),
@@ -564,7 +561,7 @@
             flops=10**9, bytes_accessed=6 * 10**6, transcendentals=10**6
         ),
         name="merge",
-    )(asker_index, has_peer, replies, stats, own_out, own_top, out_global)
+    )(asker_index, has_peer, submap_ids, anchor_ok, replies, stats, packed, table, out_global)
     return frame_out, global_update
 
 

time: 108 us -> 100 us (0.926); the launches traced: 106 us -> 100 us
  Pallas kernels: 97 us -> 91.3 us
    pallas_call x1, Pallas kernels: 74.7 us -> 70.2 us  [local(): pl.pallas_call(functools.partial(exchange_kernel, block_count), in_specs=...]
    pallas_call x1 -> x0, Pallas kernels: 2.96 us -> none  [local(): pl.pallas_call(own_kernel, grid_spec=pltpu.PrefetchScalarGridSpec(num_sca...]
    pallas_call x1, Pallas kernels: 6.49 us -> 8.26 us  [local(): pl.pallas_call(merge_kernel, grid_spec=pltpu.PrefetchScalarGridSpec(num_s...]
where the time goes in v3:
time: 100 us
  Pallas kernels  91.3 us (91%)
  local copies, waits for them, and re-layouts  4.18 us (4%)
  other arithmetic  3.89 us (4%)
    pallas_call x1, Pallas kernels, local(): pl.pallas_call(functools.partial(exchange_kernel, block_count), in_specs=...  70.2 us
    pallas_call x1, Pallas kernels, local(): pl.pallas_call(front_kernel, grid_spec=pltpu.PrefetchScalarGridSpec(num_s...  12.8 us
    pallas_call x1, Pallas kernels, local(): pl.pallas_call(merge_kernel, grid_spec=pltpu.PrefetchScalarGridSpec(num_s...  8.26 us
    unnamed x14, local copies, waits for them, and re-layouts  4.01 us

profile of v3, /device:TPU:1, one launch (start us, length us, event | category | flops | bytes accessed | tf_op | source)
XLA Modules:
  0.0 100.1 jit_solution(15052837048946437158)
XLA Ops:
  0.6 0.7 compare_convert_fusion.1.holding
  1.3 0.9 select_reduce_fusion.3
  2.2 0.9 compare_reduce_fusion
  3.0 0.7 and_select_fusion.held
  3.7 0.7 fusion
  4.4 0.1 select_reduce_fusion.1
  4.6 0.1 copy.14
  4.6 0.1 reshape.58.request
  4.7 0.0 copy-start.4
  4.7 0.7 copy-done.4
  5.4 0.0 copy-start.5
  5.4 0.7 copy-done.5
  6.1 12.8 %front.1 = (bf16[8,64,1024]{2,1,0:T(8,128)(2,1)}, bf16[8,64,1536]{2,1,0:T(8,128)(2,1)}, bf16[16,64,512]{2,1,0:T(8,128)(2,1)S(1)}, f32[16,8,128]{2,1,0:T(8,128)S(1)}, bf16[64,16,512]{2,1,0:T(8,128)(2,1)}) custom-call(s32[16]{0:T(128)S(1)} %get-tuple-element.20.asker, s32[32]{0:T(128)S(1)} %reshape.58.request, s32[8]{0:T(128)S(1)} %compare_convert_fusion.1.holding, ...), custom_call_target="tpu_custom_call" | custom-call | flops 4000000000 | bytes 15000000 | tf_op jit(solution)/shard_map/front/pallas_call | solution.py:464
  18.9 0.0 copy-start
  18.9 1.4 %copy-done = bf16[8,64,1536]{2,1,0:T(8,128)(2,1)S(1)} copy-done((bf16[8,64,1536]{2,1,0:T(8,128)(2,1)S(1)}, bf16[8,64,1536]{2,1,0:T(8,128)(2,1)}, u32[]{:S(2)}) %copy-start) | copy-done | bytes 1572888
  20.3 0.0 copy-start.6
  20.3 1.2 %copy-done.6 = bf16[64,16,512]{2,1,0:T(8,128)(2,1)S(1)} copy-done((bf16[64,16,512]{2,1,0:T(8,128)(2,1)S(1)}, bf16[64,16,512]{2,1,0:T(8,128)(2,1)}, u32[]{:S(2)}) %copy-start.6) | copy-done | bytes 1048600
  21.6 0.0 copy-start.1
  21.6 0.0 copy-start.2
  21.6 0.0 copy-start.3
  21.6 70.2 %exchange.1 = (bf16[16,64,512]{2,1,0:T(8,128)(2,1)S(1)}, f32[16,8,128]{2,1,0:T(8,128)S(1)}, bf16[64,16,512]{2,1,0:T(8,128)(2,1)S(1)}) custom-call(bf16[16,64,512]{2,1,0:T(8,128)(2,1)S(1)} %get-tuple-element.11.queries, f32[16,8,128]{2,1,0:T(8,128)S(1)} %get-tuple-element.12.notes, bf16[8,64,1536]{2,1,0:T(8,128)(2,1)S(1)} %copy-done, ...), custom_call_target="tpu_custom_call" | custom-call | flops 4000000000 | bytes 8000000 | tf_op jit(solution)/shard_map/exchange/pallas_call | solution.py:513
  91.8 0.0 copy-done.1
  91.8 0.0 copy-done.2
  91.8 0.0 copy-done.3
  91.8 8.3 %merge.1 = bf16[8,64,1024]{2,1,0:T(8,128)(2,1)} custom-call(s32[16]{0:T(128)S(1)} %get-tuple-element.20.asker, s32[16]{0:T(128)S(1)} %compare_convert_fusion.has_peer, s32[8]{0:T(128)S(1)} %copy-done.3, s32[8]{0:T(128)S(1)} %and_convert_fusion.anchor_ok, bf16[16,64,512]{2,1,0:T(8,128)(2,1)S(1)} %get-tuple-element.15.replies, ...), custom_call_target="tpu_custom_call" | custom-call | flops 1000000000 | bytes 6000000 | tf_op jit(solution)/shard_map/merge/pallas_call | solution.py:542
  (4 shorter events, 0.0 us)
Async XLA Ops:
  4.7 0.7 copy-start.4
  5.4 0.7 copy-start.5
  18.9 1.4 %copy-start = (bf16[8,64,1536]{2,1,0:T(8,128)(2,1)S(1)}, bf16[8,64,1536]{2,1,0:T(8,128)(2,1)}, u32[]{:S(2)}) copy-start(bf16[8,64,1536]{2,1,0:T(8,128)(2,1)} %get-tuple-element.13.packed) | copy-start | bytes 4718596
  20.3 1.2 %copy-start.6 = (bf16[64,16,512]{2,1,0:T(8,128)(2,1)S(1)}, bf16[64,16,512]{2,1,0:T(8,128)(2,1)}, u32[]{:S(2)}) copy-start(bf16[64,16,512]{2,1,0:T(8,128)(2,1)} %get-tuple-element.14.anchors) | copy-start | bytes 3145732
  21.6 70.3 %copy-start.1 = (bf16[8,64,1536]{2,1,0:T(8,128)(2,1)S(1)}, bf16[8,64,1536]{2,1,0:T(8,128)(2,1)}, u32[]{:S(2)}) copy-start(bf16[8,64,1536]{2,1,0:T(8,128)(2,1)} %get-tuple-element.13.packed) | copy-start | bytes 4718596
  21.6 70.3 %copy-start.2 = (bf16[512,1024]{1,0:T(8,128)(2,1)S(1)}, bf16[512,1024]{1,0:T(8,128)(2,1)}, u32[]{:S(2)}) copy-start(bf16[512,1024]{1,0:T(8,128)(2,1)} %out_global.1) | copy-start | bytes 3145732
  21.6 70.3 %copy-start.3 = (s32[8]{0:T(128)S(1)}, s32[8]{0:T(128)}, u32[]{:S(2)}) copy-start(s32[8]{0:T(128)} %submap.1) | copy-start | bytes 100

commit v4 on v3

--- a/solution.py
+++ b/solution.py
@@ -225,8 +225,7 @@
     base = me * 0
     size = pieces
     bounds = [1 + (n - 1) * i // stages for i in range(stages + 1)]
-    later = max(stages - 1, 1)
-    asks = [1] + [1 + n // 2 + (n // 2 - 1) * i // later for i in range(stages)]
+    asks = [1] + [n - (n >> (i + 2)) for i in range(stages)]
     for i in range(stages):
         half = size // 2
         bit = (me // 2**i) % 2

time: 100 us -> 97.1 us (0.971)
  Pallas kernels: 91.3 us -> 88 us
    pallas_call x1, Pallas kernels: 70.2 us -> 66.9 us  [local(): pl.pallas_call(functools.partial(exchange_kernel, block_count), in_specs=...]
where the time goes in v4:
time: 97.1 us; the launch traced here: 96.8 us
  Pallas kernels  88 us (91%)
  local copies, waits for them, and re-layouts  4.18 us (4%)
  other arithmetic  3.89 us (4%)
    pallas_call x1, Pallas kernels, local(): pl.pallas_call(functools.partial(exchange_kernel, block_count), in_specs=...  66.9 us
    pallas_call x1, Pallas kernels, local(): pl.pallas_call(front_kernel, grid_spec=pltpu.PrefetchScalarGridSpec(num_s...  12.8 us
    pallas_call x1, Pallas kernels, local(): pl.pallas_call(merge_kernel, grid_spec=pltpu.PrefetchScalarGridSpec(num_s...  8.26 us
    unnamed x14, local copies, waits for them, and re-layouts  4.01 us

profile of v4, /device:TPU:1, one launch (start us, length us, event | category | flops | bytes accessed | tf_op | source)
XLA Modules:
  0.0 96.8 jit_solution(11652663776358071808)
XLA Ops:
  0.6 0.7 compare_convert_fusion.1.holding
  1.3 0.9 select_reduce_fusion.3
  2.2 0.9 compare_reduce_fusion
  3.0 0.7 and_select_fusion.held
  3.7 0.7 fusion
  4.4 0.1 select_reduce_fusion.1
  4.6 0.1 copy.14
  4.6 0.1 reshape.58.request
  4.7 0.0 copy-start.4
  4.7 0.7 copy-done.4
  5.4 0.0 copy-start.5
  5.4 0.7 copy-done.5
  6.1 12.8 %front.1 = (bf16[8,64,1024]{2,1,0:T(8,128)(2,1)}, bf16[8,64,1536]{2,1,0:T(8,128)(2,1)}, bf16[16,64,512]{2,1,0:T(8,128)(2,1)S(1)}, f32[16,8,128]{2,1,0:T(8,128)S(1)}, bf16[64,16,512]{2,1,0:T(8,128)(2,1)}) custom-call(s32[16]{0:T(128)S(1)} %get-tuple-element.20.asker, s32[32]{0:T(128)S(1)} %reshape.58.request, s32[8]{0:T(128)S(1)} %compare_convert_fusion.1.holding, ...), custom_call_target="tpu_custom_call" | custom-call | flops 4000000000 | bytes 15000000 | tf_op jit(solution)/shard_map/front/pallas_call | solution.py:463
  18.9 0.0 copy-start
  18.9 1.4 %copy-done = bf16[8,64,1536]{2,1,0:T(8,128)(2,1)S(1)} copy-done((bf16[8,64,1536]{2,1,0:T(8,128)(2,1)S(1)}, bf16[8,64,1536]{2,1,0:T(8,128)(2,1)}, u32[]{:S(2)}) %copy-start) | copy-done | bytes 1572888
  20.3 0.0 copy-start.6
  20.3 1.2 %copy-done.6 = bf16[64,16,512]{2,1,0:T(8,128)(2,1)S(1)} copy-done((bf16[64,16,512]{2,1,0:T(8,128)(2,1)S(1)}, bf16[64,16,512]{2,1,0:T(8,128)(2,1)}, u32[]{:S(2)}) %copy-start.6) | copy-done | bytes 1048600
  21.6 0.0 copy-start.1
  21.6 0.0 copy-start.2
  21.6 0.0 copy-start.3
  21.6 66.9 %exchange.1 = (bf16[16,64,512]{2,1,0:T(8,128)(2,1)S(1)}, f32[16,8,128]{2,1,0:T(8,128)S(1)}, bf16[64,16,512]{2,1,0:T(8,128)(2,1)S(1)}) custom-call(bf16[16,64,512]{2,1,0:T(8,128)(2,1)S(1)} %get-tuple-element.11.queries, f32[16,8,128]{2,1,0:T(8,128)S(1)} %get-tuple-element.12.notes, bf16[8,64,1536]{2,1,0:T(8,128)(2,1)S(1)} %copy-done, ...), custom_call_target="tpu_custom_call" | custom-call | flops 4000000000 | bytes 8000000 | tf_op jit(solution)/shard_map/exchange/pallas_call | solution.py:512
  88.5 0.0 copy-done.1
  88.5 0.0 copy-done.2
  88.5 0.0 copy-done.3
  88.5 8.3 %merge.1 = bf16[8,64,1024]{2,1,0:T(8,128)(2,1)} custom-call(s32[16]{0:T(128)S(1)} %get-tuple-element.20.asker, s32[16]{0:T(128)S(1)} %compare_convert_fusion.has_peer, s32[8]{0:T(128)S(1)} %copy-done.3, s32[8]{0:T(128)S(1)} %and_convert_fusion.anchor_ok, bf16[16,64,512]{2,1,0:T(8,128)(2,1)S(1)} %get-tuple-element.15.replies, ...), custom_call_target="tpu_custom_call" | custom-call | flops 1000000000 | bytes 6000000 | tf_op jit(solution)/shard_map/merge/pallas_call | solution.py:541
  (4 shorter events, 0.0 us)
Async XLA Ops:
  4.7 0.7 copy-start.4
  5.4 0.7 copy-start.5
  18.9 1.4 %copy-start = (bf16[8,64,1536]{2,1,0:T(8,128)(2,1)S(1)}, bf16[8,64,1536]{2,1,0:T(8,128)(2,1)}, u32[]{:S(2)}) copy-start(bf16[8,64,1536]{2,1,0:T(8,128)(2,1)} %get-tuple-element.13.packed) | copy-start | bytes 4718596
  20.3 1.2 %copy-start.6 = (bf16[64,16,512]{2,1,0:T(8,128)(2,1)S(1)}, bf16[64,16,512]{2,1,0:T(8,128)(2,1)}, u32[]{:S(2)}) copy-start(bf16[64,16,512]{2,1,0:T(8,128)(2,1)} %get-tuple-element.14.anchors) | copy-start | bytes 3145732
  21.6 66.9 %copy-start.1 = (bf16[8,64,1536]{2,1,0:T(8,128)(2,1)S(1)}, bf16[8,64,1536]{2,1,0:T(8,128)(2,1)}, u32[]{:S(2)}) copy-start(bf16[8,64,1536]{2,1,0:T(8,128)(2,1)} %get-tuple-element.13.packed) | copy-start | bytes 4718596
  21.6 66.9 %copy-start.2 = (bf16[512,1024]{1,0:T(8,128)(2,1)S(1)}, bf16[512,1024]{1,0:T(8,128)(2,1)}, u32[]{:S(2)}) copy-start(bf16[512,1024]{1,0:T(8,128)(2,1)} %out_global.1) | copy-start | bytes 3145732
  21.6 66.9 %copy-start.3 = (s32[8]{0:T(128)S(1)}, s32[8]{0:T(128)}, u32[]{:S(2)}) copy-start(s32[8]{0:T(128)} %submap.1) | copy-start | bytes 100
